TPU v7x, 32 devices: a whole 2x2x4 slice. The times are simulated.
32 devices in a mesh: grp: 2 (over y), gx: 4 (over z), gy: 2 (over x), gz: 2 (over core).
Axes of the slice: x: 2, y: 2, z: 4, core: 2. Of those that a mesh axis runs over, the one named last changes fastest.
Arguments:
- coef_start: float32 [81, 8, 2, 2, 128], P(None, ('grp', 'gx'), 'gy', 'gz'), parts along dimension 1, may hold values from -6 to 6
- dipole_start: float32 [3, 8, 2, 2, 128], P(None, ('grp', 'gx'), 'gy', 'gz'), parts along dimension 1, may hold values from -4 to 4
- source: float32 [81, 8, 2, 2, 128], P(None, ('grp', 'gx'), 'gy', 'gz'), parts along dimension 1, may hold values from -6 to 6
- indicator: float32 [302, 8, 2, 2, 128], P(None, ('grp', 'gx'), 'gy', 'gz'), parts along dimension 1, may hold values from 0 to 1
- polarity: float32 [8, 2, 2, 128], P(('grp', 'gx'), 'gy', 'gz'), parts along dimension 0, may hold values from 0.2 to 1
- external: float32 [3, 8, 2, 2, 128], P(None, ('grp', 'gx'), 'gy', 'gz'), parts along dimension 1, may hold values from -6 to 6
- counts: int32 [8, 2, 2], P(('grp', 'gx'), 'gy', 'gz'), parts along dimension 0, may hold values from 32 to 128, as said below
- cosmo_index: int32 [16, 8, 2, 2, 128], P(None, ('grp', 'gx'), 'gy', 'gz'), parts along dimension 1, may hold values from 0 to 991
- cosmo_weight: float32 [16, 8, 2, 2, 128], P(None, ('grp', 'gx'), 'gy', 'gz'), parts along dimension 1, may hold values from 0 to 0.08
- cosmo_dist: float32 [16, 8, 2, 2, 128], P(None, ('grp', 'gx'), 'gy', 'gz'), parts along dimension 1, may hold values from 1 to 3
- cosmo_theta: float32 [16, 8, 2, 2, 128], P(None, ('grp', 'gx'), 'gy', 'gz'), parts along dimension 1, may hold values from 0 to 3.14159
- cosmo_phi: float32 [16, 8, 2, 2, 128], P(None, ('grp', 'gx'), 'gy', 'gz'), parts along dimension 1, may hold values from -3.140625 to 3.140625
- thole_index: int32 [16, 8, 2, 2, 128], P(None, ('grp', 'gx'), 'gy', 'gz'), parts along dimension 1, may hold values from 0 to 991
- thole_weight: float32 [16, 8, 2, 2, 128], P(None, ('grp', 'gx'), 'gy', 'gz'), parts along dimension 1, may hold values from 0 to 0.5
- thole_dist: float32 [16, 8, 2, 2, 128], P(None, ('grp', 'gx'), 'gy', 'gz'), parts along dimension 1, may hold values from 1 to 3
- thole_theta: float32 [16, 8, 2, 2, 128], P(None, ('grp', 'gx'), 'gy', 'gz'), parts along dimension 1, may hold values from 0 to 3.14159
- thole_phi: float32 [16, 8, 2, 2, 128], P(None, ('grp', 'gx'), 'gy', 'gz'), parts along dimension 1, may hold values from -3.140625 to 3.140625
- harmonics: float32 [302, 81], replicated, may hold values from -6 to 6
- lebedev: float32 [302], replicated, may hold values from 0.03 to 0.055
Outputs:
- coefficients: float32 [81, 8, 2, 2, 128], P(None, ('grp', 'gx'), 'gy', 'gz'), parts along dimension 1
- dipoles: float32 [3, 8, 2, 2, 128], P(None, ('grp', 'gx'), 'gy', 'gz'), parts along dimension 1
There are 2 independent parts, one for each index of `grp`. A program takes and returns all parts, laid end to end along the dimension named above; an argument that names none is the same for every part. Nothing has to cross between parts.
Inputs may be any that keep to these rules, and one draw needn't show every extreme that they name: `counts`: the live spheres of a domain are its leading slots and include all 32 slots that neighbours may reference; some domain is full and some holds only 32.
All inputs are finite; a program needn't handle non-finite values.
Results may differ from a plain program's by a relative error of at most 0.0003.
Values sent between devices are 32-bit elements; how exact they have to be, the bound alone decides.
A program may use at most 64 MiB of HBM per device.

v0:
```python
import math

import jax
import jax.numpy as jnp
from jax import lax
from jax.sharding import PartitionSpec as P

ITERS = 3


PRECISE = lax.Precision.HIGHEST
THOLE_DAMPING = 0.39
INJECT_SCALE = 2.0
RADIUS_SCALE = 0.9


def extended_2(block, sides, width):
    for axis, dim in sides:
        count = lax.axis_size(axis)
        forward = [(i, i + 1) for i in range(count - 1)]
        backward = [(target, source) for source, target in forward]
        low = lax.ppermute(
            lax.slice_in_dim(block, block.shape[dim] - width, None, axis=dim), axis, forward
        )
        high = lax.ppermute(lax.slice_in_dim(block, 0, width, axis=dim), axis, backward)
        block = jnp.concatenate([low, block, high], axis=dim)
    return block


def degree_table(coef_total):
    row_index = jnp.arange(coef_total)
    squares = jnp.arange(1, math.isqrt(coef_total)) ** 2
    return jnp.sum((row_index[:, None] >= squares[None, :]).astype(jnp.float32), axis=1)


def unit_vectors(polar_angle, azimuth):
    sin_theta = jnp.sin(polar_angle)
    return jnp.stack(
        [sin_theta * jnp.cos(azimuth), sin_theta * jnp.sin(azimuth), jnp.cos(polar_angle)]
    )


def domain_update(
    candidates,
    coeffs,
    dipoles,
    source,
    indicator,
    cosmo_index,
    cosmo_weight,
    cosmo_dist,
    cosmo_theta,
    cosmo_phi,
    thole_index,
    thole_weight,
    thole_dist,
    thole_theta,
    thole_phi,
    harmonics,
    lebedev,
    living,
):
    coef_count = coeffs.shape[0]
    sphere_count = coeffs.shape[1]
    degree_rows = degree_table(coef_count)
    neighbours = jnp.take(candidates[:coef_count], cosmo_index, axis=1)
    ratio_log = jnp.log(RADIUS_SCALE / cosmo_dist)
    radial = jnp.exp(degree_rows[:, None, None] * ratio_log[None])
    coupled = jnp.sum(cosmo_weight[None] * radial * neighbours, axis=1)
    stacked = jnp.concatenate([coupled, coeffs], axis=1)
    values = jnp.dot(harmonics, stacked, precision=PRECISE, preferred_element_type=jnp.float32)
    density = lebedev[:, None] * indicator
    weighted = values * jnp.concatenate([density, density], axis=1)
    projected = lax.dot_general(
        harmonics,
        weighted,
        (((0,), (0,)), ((), ())),
        precision=PRECISE,
        preferred_element_type=jnp.float32,
    )
    scaled = (2.0 * degree_rows + 1.0) / (4.0 * math.pi)
    injected = source + jnp.pad(INJECT_SCALE * dipoles, ((1, coef_count - 4), (0, 0)))
    new_coeffs = living[None, :] * scaled[:, None] * (injected - projected[:, :sphere_count])
    moment = projected[1:4, sphere_count:]
    cosmo_dirs = unit_vectors(cosmo_theta, cosmo_phi)
    along_axis = jnp.sum(cosmo_dirs * moment[:, None, :], axis=0)
    strength = cosmo_weight / cosmo_dist**3
    partial_field = strength[None] * (3.0 * cosmo_dirs * along_axis[None] - moment[:, None, :])
    flat_field = partial_field.reshape(3, -1).T
    pushed = jax.ops.segment_sum(
        flat_field, cosmo_index.reshape(-1), num_segments=candidates.shape[1]
    ).T
    partner = jnp.take(candidates[coef_count:], thole_index, axis=1)
    thole_dirs = unit_vectors(thole_theta, thole_phi)
    dist_cubed = thole_dist**3
    screen = jnp.exp(-THOLE_DAMPING * dist_cubed)
    lambda_three = 1.0 - screen
    lambda_five = 1.0 - (1.0 + THOLE_DAMPING * dist_cubed) * screen
    projection = jnp.sum(thole_dirs * partner, axis=0)
    tensor_part = (
        3.0 * lambda_five[None] * thole_dirs * projection[None] - lambda_three[None] * partner
    )
    induced = jnp.sum((thole_weight / dist_cubed)[None] * tensor_part, axis=1)
    return (new_coeffs, pushed, induced)


def flatten_rows(values_in):
    return values_in.reshape(values_in.shape[0], values_in.shape[-1])


def spread_blocks(outward):
    return extended_2(outward, (("gx", 1), ("gy", 2), ("gz", 3)), 1)


def collect_fields(partials):
    extended = extended_2(partials, (("gx", 1),), 1)
    reduced = extended[:, 0] + extended[:, 2] + extended[:, 4]
    extended = extended_2(reduced, (("gy", 1),), 1)
    reduced = extended[:, 0] + extended[:, 2] + extended[:, 4]
    extended = extended_2(reduced, (("gz", 1),), 1)
    return extended[:, 0] + extended[:, 2] + extended[:, 4]


def local(
    coef_start,
    dipole_start,
    source,
    indicator,
    polarity,
    external,
    counts,
    cosmo_index,
    cosmo_weight,
    cosmo_dist,
    cosmo_theta,
    cosmo_phi,
    thole_index,
    thole_weight,
    thole_dist,
    thole_theta,
    thole_phi,
    harmonics,
    lebedev,
):
    coef_count = coef_start.shape[0]
    sphere_count = coef_start.shape[4]
    border_count = sphere_count // 4
    state_rows = coef_count + 3
    living = (jnp.arange(sphere_count, dtype=jnp.int32) < counts.reshape(())).astype(jnp.float32)
    polar_flat = polarity.reshape(sphere_count)
    source_flat = flatten_rows(source)
    indicator_flat = flatten_rows(indicator)
    external_flat = flatten_rows(external)
    cindex_flat = flatten_rows(cosmo_index)
    cweight_flat = flatten_rows(cosmo_weight)
    cdist_flat = flatten_rows(cosmo_dist)
    ctheta_flat = flatten_rows(cosmo_theta)
    cphi_flat = flatten_rows(cosmo_phi)
    tindex_flat = flatten_rows(thole_index)
    tweight_flat = flatten_rows(thole_weight)
    tdist_flat = flatten_rows(thole_dist)
    ttheta_flat = flatten_rows(thole_theta)
    tphi_flat = flatten_rows(thole_phi)
    coeffs = flatten_rows(coef_start)
    dipoles = flatten_rows(dipole_start)
    for sweep_index in range(ITERS):
        current = jnp.concatenate([coeffs, dipoles], axis=0)
        outward = current[:, :border_count].reshape(state_rows, 1, 1, 1, border_count)
        nearby = spread_blocks(outward)
        candidates = jnp.concatenate(
            [nearby.reshape(state_rows, 27 * border_count), current], axis=1
        )
        new_coeffs, pushed, induced = domain_update(
            candidates,
            coeffs,
            dipoles,
            source_flat,
            indicator_flat,
            cindex_flat,
            cweight_flat,
            cdist_flat,
            ctheta_flat,
            cphi_flat,
            tindex_flat,
            tweight_flat,
            tdist_flat,
            ttheta_flat,
            tphi_flat,
            harmonics,
            lebedev,
            living,
        )
        returned = collect_fields(pushed[:, : 27 * border_count].reshape(3, 3, 3, 3, border_count))
        field_back = pushed[:, 27 * border_count :] + jnp.pad(
            returned, ((0, 0), (0, sphere_count - border_count))
        )
        dipoles = living[None, :] * polar_flat[None, :] * (external_flat + induced + field_back)
        coeffs = new_coeffs
    return (coeffs.reshape(coef_start.shape), dipoles.reshape(dipole_start.shape))


def solution(mesh):
    in_specs = (
        P(None, ("grp", "gx"), "gy", "gz", None),
        P(None, ("grp", "gx"), "gy", "gz", None),
        P(None, ("grp", "gx"), "gy", "gz", None),
        P(None, ("grp", "gx"), "gy", "gz", None),
        P(("grp", "gx"), "gy", "gz", None),
        P(None, ("grp", "gx"), "gy", "gz", None),
        P(("grp", "gx"), "gy", "gz"),
        P(None, ("grp", "gx"), "gy", "gz", None),
        P(None, ("grp", "gx"), "gy", "gz", None),
        P(None, ("grp", "gx"), "gy", "gz", None),
        P(None, ("grp", "gx"), "gy", "gz", None),
        P(None, ("grp", "gx"), "gy", "gz", None),
        P(None, ("grp", "gx"), "gy", "gz", None),
        P(None, ("grp", "gx"), "gy", "gz", None),
        P(None, ("grp", "gx"), "gy", "gz", None),
        P(None, ("grp", "gx"), "gy", "gz", None),
        P(None, ("grp", "gx"), "gy", "gz", None),
        P(),
        P(),
    )
    out_specs = (P(None, ("grp", "gx"), "gy", "gz", None), P(None, ("grp", "gx"), "gy", "gz", None))
    return jax.shard_map(local, mesh=mesh, in_specs=in_specs, out_specs=out_specs, check_vma=False)
```

profile of v0, /device:TPU:0, one launch (start us, length us, event | category | flops | bytes accessed | tf_op | source)
XLA Modules:
  0.0 201.4 jit_solution(1964080766847201147)
XLA Ops:
  1.8 5.0 %collective-permute-start = (f32[84,1,1,1,32]{0,4,3,2,1:T(8,128)S(1)}, f32[84,1,1,1,32]{0,4,3,2,1:T(8,128)S(1)}, u32[]{:S(2)}, u32[]{:S(2)}) collective-permute-start(f32[84,1,1,1,32]{0,4,3,2,1:T(8,128)S(1)} %fusion.50), channel_id=1, source_target_pairs={{0,4},{4,8},{8,12},{1,5},{5,9},{9,13},{2,6},{6,10},{10,14},{3,7},{... | collective-permute-start | bytes 32264 | tf_op jit(solution)/shard_map/ppermute | solution.py:22
  6.9 1.3 collective-permute-start.1
  13.0 3.4 %collective-permute-start.2 = (f32[84,3,1,1,32]{0,4,3,2,1:T(8,128)S(1)}, f32[84,3,1,1,32]{0,4,3,2,1:T(8,128)S(1)}, u32[]{:S(2)}, u32[]{:S(2)}) collective-permute-start(f32[84,3,1,1,32]{0,4,3,2,1:T(8,128)S(1)} %pad_maximum_fusion.11), channel_id=1, source_target_pairs={{0,2},{1,3},{4,6},{5,7},{8,10},{9,11},{12,14},{13,15},{16,18},{17,... | collective-permute-start | bytes 96776 | tf_op jit(solution)/shard_map/ppermute | solution.py:22
  16.4 1.3 collective-permute-start.3
  18.1 4.3 %collective-permute-done.3 = f32[84,3,1,1,32]{0,4,3,2,1:T(8,128)S(1)} collective-permute-done((f32[84,3,1,1,32]{0,4,3,2,1:T(8,128)S(1)}, f32[84,3,1,1,32]{0,4,3,2,1:T(8,128)S(1)}, u32[]{:S(2)}, u32[]{:S(2)}) %collective-permute-start.3) | collective-permute-done | bytes 32288 | tf_op jit(solution)/shard_map/ppermute | solution.py:25
  22.4 1.3 collective-permute-start.4
  23.7 1.3 collective-permute-start.5
  25.0 1.9 collective-permute-done.5
  27.1 5.5 %gather_fusion = f32[2048,81]{1,0:T(8,128)S(1)} fusion(f32[81,992]{0,1:T(8,128)S(1)} %bitcast.220, s32[2048]{0:T(1024)S(1)} %bitcast_clamp_fusion.1), kind=kCustom, calls=%fused_computation.clone | custom fusion | bytes 1335296 | tf_op jit(solution)/shard_map/jit(_take)/gather | solution.py:66
  34.9 11.6 %scatter_custom_fusion = f32[992,3]{1,0:T(8,128)S(1)} fusion(s32[2048]{0:T(1024)S(1)} %bitcast.281, f32[2048,3]{1,0:T(8,128)S(1)} %copy.144, f32[]{:T(128)} %constant.26.clone.1), kind=kCustom, calls=%fused_computation.38 | custom fusion | flops 6144 | bytes 11908 | tf_op jit(solution)/shard_map/scatter-add | solution.py:90
  46.9 4.5 %collective-permute-start.6 = (f32[3,1,3,3,32]{4,0,3,2,1:T(4,128)S(1)}, f32[3,1,3,3,32]{4,0,3,2,1:T(4,128)S(1)}, u32[]{:S(2)}, u32[]{:S(2)}) collective-permute-start(f32[3,1,3,3,32]{4,0,3,2,1:T(4,128)S(1)} %copy.177), channel_id=1, source_target_pairs={{0,4},{4,8},{8,12},{1,5},{5,9},{9,13},{2,6},{6,10},{10,14},{3,7},{... | collective-permute-start | bytes 10376 | tf_op jit(solution)/shard_map/ppermute | solution.py:22
  53.0 5.5 %gather_fusion.1 = f32[2048,3]{1,0:T(8,128)S(1)} fusion(f32[3,992]{0,1:T(8,128)S(1)} %slice.206, s32[2048]{0:T(1024)S(1)} %bitcast_clamp_fusion), kind=kCustom, calls=%fused_computation.1.clone | custom fusion | bytes 57344 | tf_op jit(solution)/shard_map/jit(_take)/gather | solution.py:93
  58.9 1.6 collective-permute-start.8
  60.5 1.3 collective-permute-start.9
  61.8 4.2 %collective-permute-done.9 = f32[3,1,3,32]{3,0,2,1:T(4,128)S(1)} collective-permute-done((f32[3,1,3,32]{3,0,2,1:T(4,128)S(1)}, f32[3,1,3,32]{3,0,2,1:T(4,128)S(1)}, u32[]{:S(2)}, u32[]{:S(2)}) %collective-permute-start.9) | collective-permute-done | bytes 1184 | tf_op jit(solution)/shard_map/ppermute | solution.py:25
  68.6 1.7 collective-permute-done.11
  70.4 4.6 %collective-permute-start.12 = (f32[84,1,1,1,32]{4,0,3,2,1:T(8,128)S(1)}, f32[84,1,1,1,32]{4,0,3,2,1:T(8,128)S(1)}, u32[]{:S(2)}, u32[]{:S(2)}) collective-permute-start(f32[84,1,1,1,32]{4,0,3,2,1:T(8,128)S(1)} %fusion.24), channel_id=1, source_target_pairs={{0,4},{4,8},{8,12},{1,5},{5,9},{9,13},{2,6},{6,10},{10,14},{3,7},{... | collective-permute-start | bytes 32264 | tf_op jit(solution)/shard_map/ppermute | solution.py:22
  76.8 4.2 %collective-permute-done.13 = f32[84,1,1,1,32]{4,0,3,2,1:T(8,128)S(1)} collective-permute-done((f32[84,1,1,1,32]{4,0,3,2,1:T(8,128)S(1)}, f32[84,1,1,1,32]{4,0,3,2,1:T(8,128)S(1)}, u32[]{:S(2)}, u32[]{:S(2)}) %collective-permute-start.13) | collective-permute-done | bytes 10784 | tf_op jit(solution)/shard_map/ppermute | solution.py:25
  81.0 1.6 collective-permute-start.14
  82.7 1.3 collective-permute-start.15
  84.4 4.3 %collective-permute-done.15 = f32[84,3,1,1,32]{0,4,3,2,1:T(8,128)S(1)} collective-permute-done((f32[84,3,1,1,32]{0,4,3,2,1:T(8,128)S(1)}, f32[84,3,1,1,32]{0,4,3,2,1:T(8,128)S(1)}, u32[]{:S(2)}, u32[]{:S(2)}) %collective-permute-start.15) | collective-permute-done | bytes 32288 | tf_op jit(solution)/shard_map/ppermute | solution.py:25
  88.7 1.3 collective-permute-start.16
  91.4 1.8 collective-permute-done.17
  93.3 5.5 %gather_fusion.3 = f32[2048,81]{1,0:T(8,128)S(1)} fusion(f32[81,992]{0,1:T(8,128)S(1)} %pad_maximum_fusion.1, s32[2048]{0:T(1024)S(1)} %bitcast_clamp_fusion.1), kind=kCustom, calls=%fused_computation.2.clone | custom fusion | bytes 1335296 | tf_op jit(solution)/shard_map/jit(_take)/gather | solution.py:66
  101.2 11.6 %scatter_custom_fusion.1 = f32[992,3]{1,0:T(8,128)S(1)} fusion(s32[2048]{0:T(1024)S(1)} %bitcast.282, f32[2048,3]{1,0:T(8,128)S(1)} %copy.155, f32[]{:T(128)} %constant.26.clone.1), kind=kCustom, calls=%fused_computation.36 | custom fusion | flops 6144 | bytes 11908 | tf_op jit(solution)/shard_map/scatter-add | solution.py:90
  113.1 3.5 %collective-permute-start.18 = (f32[3,1,3,3,32]{4,0,3,2,1:T(4,128)S(1)}, f32[3,1,3,3,32]{4,0,3,2,1:T(4,128)S(1)}, u32[]{:S(2)}, u32[]{:S(2)}) collective-permute-start(f32[3,1,3,3,32]{4,0,3,2,1:T(4,128)S(1)} %copy.180), channel_id=1, source_target_pairs={{0,4},{4,8},{8,12},{1,5},{5,9},{9,13},{2,6},{6,10},{10,14},{3,7},{... | collective-permute-start | bytes 10376 | tf_op jit(solution)/shard_map/ppermute | solution.py:22
  116.7 1.3 collective-permute-start.19
  118.2 5.5 %gather_fusion.2 = f32[2048,3]{1,0:T(8,128)S(1)} fusion(f32[3,992]{0,1:T(8,128)S(1)} %slice_maximum_fusion.1, s32[2048]{0:T(1024)S(1)} %bitcast_clamp_fusion), kind=kCustom, calls=%fused_computation.4.clone | custom fusion | bytes 57344 | tf_op jit(solution)/shard_map/jit(_take)/gather | solution.py:93
  124.1 1.6 collective-permute-start.20
  127.0 4.2 %collective-permute-done.21 = f32[3,1,3,32]{3,0,2,1:T(4,128)S(1)} collective-permute-done((f32[3,1,3,32]{3,0,2,1:T(4,128)S(1)}, f32[3,1,3,32]{3,0,2,1:T(4,128)S(1)}, u32[]{:S(2)}, u32[]{:S(2)}) %collective-permute-start.21) | collective-permute-done | bytes 1184 | tf_op jit(solution)/shard_map/ppermute | solution.py:25
  132.5 1.3 collective-permute-start.23
  133.9 1.7 collective-permute-done.23
  135.7 4.6 %collective-permute-start.24 = (f32[84,1,1,1,32]{4,0,3,2,1:T(8,128)S(1)}, f32[84,1,1,1,32]{4,0,3,2,1:T(8,128)S(1)}, u32[]{:S(2)}, u32[]{:S(2)}) collective-permute-start(f32[84,1,1,1,32]{4,0,3,2,1:T(8,128)S(1)} %fusion.22), channel_id=1, source_target_pairs={{0,4},{4,8},{8,12},{1,5},{5,9},{9,13},{2,6},{6,10},{10,14},{3,7},{... | collective-permute-start | bytes 32264 | tf_op jit(solution)/shard_map/ppermute | solution.py:22
  140.2 1.3 collective-permute-start.25
  142.0 4.2 %collective-permute-done.25 = f32[84,1,1,1,32]{4,0,3,2,1:T(8,128)S(1)} collective-permute-done((f32[84,1,1,1,32]{4,0,3,2,1:T(8,128)S(1)}, f32[84,1,1,1,32]{4,0,3,2,1:T(8,128)S(1)}, u32[]{:S(2)}, u32[]{:S(2)}) %collective-permute-start.25) | collective-permute-done | bytes 10784 | tf_op jit(solution)/shard_map/ppermute | solution.py:25
  146.2 1.6 collective-permute-start.26
  147.9 1.5 collective-permute-start.27
  149.6 4.3 %collective-permute-done.27 = f32[84,3,1,1,32]{0,4,3,2,1:T(8,128)S(1)} collective-permute-done((f32[84,3,1,1,32]{0,4,3,2,1:T(8,128)S(1)}, f32[84,3,1,1,32]{0,4,3,2,1:T(8,128)S(1)}, u32[]{:S(2)}, u32[]{:S(2)}) %collective-permute-start.27) | collective-permute-done | bytes 32288 | tf_op jit(solution)/shard_map/ppermute | solution.py:25
  153.9 1.3 collective-permute-start.28
  156.6 1.8 collective-permute-done.29
  158.6 5.5 %gather_fusion.4 = f32[2048,81]{1,0:T(8,128)S(1)} fusion(f32[81,992]{0,1:T(8,128)S(1)} %slice_maximum_fusion, s32[2048]{0:T(1024)S(1)} %bitcast_clamp_fusion.1), kind=kCustom, calls=%fused_computation.3.clone | custom fusion | bytes 1335296 | tf_op jit(solution)/shard_map/jit(_take)/gather | solution.py:66
  166.4 11.6 %scatter_custom_fusion.2 = f32[992,3]{1,0:T(8,128)S(1)} fusion(s32[2048]{0:T(1024)S(1)} %bitcast.283, f32[2048,3]{1,0:T(8,128)S(1)} %copy.166, f32[]{:T(128)} %constant.26.clone.1), kind=kCustom, calls=%fused_computation.34 | custom fusion | flops 6144 | bytes 11908 | tf_op jit(solution)/shard_map/scatter-add | solution.py:90
  178.4 3.5 %collective-permute-start.30 = (f32[3,1,3,3,32]{4,0,3,2,1:T(4,128)S(1)}, f32[3,1,3,3,32]{4,0,3,2,1:T(4,128)S(1)}, u32[]{:S(2)}, u32[]{:S(2)}) collective-permute-start(f32[3,1,3,3,32]{4,0,3,2,1:T(4,128)S(1)} %copy.183), channel_id=1, source_target_pairs={{0,4},{4,8},{8,12},{1,5},{5,9},{9,13},{2,6},{6,10},{10,14},{3,7},{... | collective-permute-start | bytes 10376 | tf_op jit(solution)/shard_map/ppermute | solution.py:22
  181.9 1.3 collective-permute-start.31
  183.5 5.5 %gather_fusion.5 = f32[2048,3]{1,0:T(8,128)S(1)} fusion(f32[3,992]{0,1:T(8,128)S(1)} %pad_maximum_fusion, s32[2048]{0:T(1024)S(1)} %bitcast_clamp_fusion), kind=kCustom, calls=%fused_computation.5.clone | custom fusion | bytes 57344 | tf_op jit(solution)/shard_map/jit(_take)/gather | solution.py:93
  189.3 1.6 collective-permute-start.32
  192.2 4.2 %collective-permute-done.33 = f32[3,1,3,32]{3,0,2,1:T(4,128)S(1)} collective-permute-done((f32[3,1,3,32]{3,0,2,1:T(4,128)S(1)}, f32[3,1,3,32]{3,0,2,1:T(4,128)S(1)}, u32[]{:S(2)}, u32[]{:S(2)}) %collective-permute-start.33) | collective-permute-done | bytes 1184 | tf_op jit(solution)/shard_map/ppermute | solution.py:25
  197.7 1.3 collective-permute-start.35
  (194 shorter events, 33.3 us)
Async XLA Ops:
  0.6 32.9 %copy-start = (f32[302,81]{0,1:T(8,128)S(1)}, f32[302,81]{0,1:T(8,128)}, u32[]{:S(2)}) copy-start(f32[302,81]{0,1:T(8,128)} %param.40) | copy-start | bytes 293548
  0.6 0.9 copy-start.14
  1.7 6.5 %copy-start.7 = (s32[16,1,1,1,128]{4,3,2,1,0:T(1,128)S(1)}, s32[16,1,1,1,128]{4,3,2,1,0:T(1,128)}, u32[]{:S(2)}) copy-start(s32[16,1,1,1,128]{4,3,2,1,0:T(1,128)} %param.35) | copy-start | bytes 24580
  1.7 6.5 %copy-start.8 = (s32[16,1,1,1,128]{4,3,2,1,0:T(1,128)S(1)}, s32[16,1,1,1,128]{4,3,2,1,0:T(1,128)}, u32[]{:S(2)}) copy-start(s32[16,1,1,1,128]{4,3,2,1,0:T(1,128)} %param.30) | copy-start | bytes 24580
  1.7 6.6 %copy-start.10 = (f32[16,1,1,1,128]{4,3,2,1,0:T(1,128)S(1)}, f32[16,1,1,1,128]{4,3,2,1,0:T(1,128)}, u32[]{:S(2)}) copy-start(f32[16,1,1,1,128]{4,3,2,1,0:T(1,128)} %param.38) | copy-start | bytes 24580
  1.7 6.6 %copy-start.4 = (f32[16,1,1,1,128]{4,3,2,1,0:T(1,128)S(1)}, f32[16,1,1,1,128]{4,3,2,1,0:T(1,128)}, u32[]{:S(2)}) copy-start(f32[16,1,1,1,128]{4,3,2,1,0:T(1,128)} %param.39) | copy-start | bytes 24580
  1.7 7.0 %copy-start.6 = (f32[16,1,1,1,128]{4,3,2,1,0:T(1,128)S(1)}, f32[16,1,1,1,128]{4,3,2,1,0:T(1,128)}, u32[]{:S(2)}) copy-start(f32[16,1,1,1,128]{4,3,2,1,0:T(1,128)} %param.32) | copy-start | bytes 24580
  1.8 9.1 %copy-start.2 = (f32[302,1,1,1,128]{4,3,2,1,0:T(1,128)S(1)}, f32[302,1,1,1,128]{4,3,2,1,0:T(1,128)}, u32[]{:S(2)}) copy-start(f32[302,1,1,1,128]{4,3,2,1,0:T(1,128)} %param.26) | copy-start | bytes 463876
  1.8 11.1 %collective-permute-start = (f32[84,1,1,1,32]{0,4,3,2,1:T(8,128)S(1)}, f32[84,1,1,1,32]{0,4,3,2,1:T(8,128)S(1)}, u32[]{:S(2)}, u32[]{:S(2)}) collective-permute-start(f32[84,1,1,1,32]{0,4,3,2,1:T(8,128)S(1)} %fusion.50), channel_id=1, source_target_pairs={{0,4},{4,8},{8,12},{1,5},{5,9},{9,13},{2,6},{6,10},{10,14},{3,7},{... | collective-permute-start | bytes 32264 | tf_op jit(solution)/shard_map/ppermute | solution.py:22
  6.9 6.1 %collective-permute-start.1 = (f32[84,1,1,1,32]{0,4,3,2,1:T(8,128)S(1)}, f32[84,1,1,1,32]{0,4,3,2,1:T(8,128)S(1)}, u32[]{:S(2)}, u32[]{:S(2)}) collective-permute-start(f32[84,1,1,1,32]{0,4,3,2,1:T(8,128)S(1)} %fusion.50), channel_id=1, source_target_pairs={{4,0},{8,4},{12,8},{5,1},{9,5},{13,9},{6,2},{10,6},{14,10},{7,3},{... | collective-permute-start | bytes 32264 | tf_op jit(solution)/shard_map/ppermute | solution.py:25
  10.2 0.7 copy-start.13
  13.0 4.7 %copy-start.16 = (f32[1,1,1,128]{3,2,1,0:T(1,128)S(1)}, f32[1,1,1,128]{3,2,1,0:T(1,128)}, u32[]{:S(2)}) copy-start(f32[1,1,1,128]{3,2,1,0:T(1,128)} %param.27) | copy-start | bytes 1540
  13.0 5.1 %collective-permute-start.2 = (f32[84,3,1,1,32]{0,4,3,2,1:T(8,128)S(1)}, f32[84,3,1,1,32]{0,4,3,2,1:T(8,128)S(1)}, u32[]{:S(2)}, u32[]{:S(2)}) collective-permute-start(f32[84,3,1,1,32]{0,4,3,2,1:T(8,128)S(1)} %pad_maximum_fusion.11), channel_id=1, source_target_pairs={{0,2},{1,3},{4,6},{5,7},{8,10},{9,11},{12,14},{13,15},{16,18},{17,... | collective-permute-start | bytes 96776 | tf_op jit(solution)/shard_map/ppermute | solution.py:22
  16.4 6.0 %collective-permute-start.3 = (f32[84,3,1,1,32]{0,4,3,2,1:T(8,128)S(1)}, f32[84,3,1,1,32]{0,4,3,2,1:T(8,128)S(1)}, u32[]{:S(2)}, u32[]{:S(2)}) collective-permute-start(f32[84,3,1,1,32]{0,4,3,2,1:T(8,128)S(1)} %pad_maximum_fusion.11), channel_id=1, source_target_pairs={{2,0},{3,1},{6,4},{7,5},{10,8},{11,9},{14,12},{15,13},{18,16},{19,... | collective-permute-start | bytes 96776 | tf_op jit(solution)/shard_map/ppermute | solution.py:25
  22.4 2.6 %collective-permute-start.4 = (f32[84,3,3,1,32]{0,4,3,2,1:T(8,128)S(1)}, f32[84,3,3,1,32]{0,4,3,2,1:T(8,128)S(1)}, u32[]{:S(2)}, u32[]{:S(2)}) collective-permute-start(f32[84,3,3,1,32]{0,4,3,2,1:T(8,128)S(1)} %pad_maximum_fusion.6), channel_id=1, source_target_pairs={{0,1},{2,3},{4,5},{6,7},{8,9},{10,11},{12,13},{14,15},{16,17},{18,... | collective-permute-start | bytes 290312 | tf_op jit(solution)/shard_map/ppermute | solution.py:22
  23.7 3.3 %collective-permute-start.5 = (f32[84,3,3,1,32]{0,4,3,2,1:T(8,128)S(1)}, f32[84,3,3,1,32]{0,4,3,2,1:T(8,128)S(1)}, u32[]{:S(2)}, u32[]{:S(2)}) collective-permute-start(f32[84,3,3,1,32]{0,4,3,2,1:T(8,128)S(1)} %pad_maximum_fusion.6), channel_id=1, source_target_pairs={{1,0},{3,2},{5,4},{7,6},{9,8},{11,10},{13,12},{15,14},{17,16},{19,... | collective-permute-start | bytes 290312 | tf_op jit(solution)/shard_map/ppermute | solution.py:25
  46.8 5.9 %copy-start.1 = (f32[81,1,1,1,128]{4,3,2,1,0:T(1,128)S(1)}, f32[81,1,1,1,128]{4,3,2,1,0:T(1,128)}, u32[]{:S(2)}) copy-start(f32[81,1,1,1,128]{4,3,2,1,0:T(1,128)} %param.25) | copy-start | bytes 124420
  46.9 12.0 %collective-permute-start.6 = (f32[3,1,3,3,32]{4,0,3,2,1:T(4,128)S(1)}, f32[3,1,3,3,32]{4,0,3,2,1:T(4,128)S(1)}, u32[]{:S(2)}, u32[]{:S(2)}) collective-permute-start(f32[3,1,3,3,32]{4,0,3,2,1:T(4,128)S(1)} %copy.177), channel_id=1, source_target_pairs={{0,4},{4,8},{8,12},{1,5},{5,9},{9,13},{2,6},{6,10},{10,14},{3,7},{... | collective-permute-start | bytes 10376 | tf_op jit(solution)/shard_map/ppermute | solution.py:22
  51.4 7.4 %collective-permute-start.7 = (f32[3,1,3,3,32]{4,0,3,2,1:T(4,128)S(1)}, f32[3,1,3,3,32]{4,0,3,2,1:T(4,128)S(1)}, u32[]{:S(2)}, u32[]{:S(2)}) collective-permute-start(f32[3,1,3,3,32]{4,0,3,2,1:T(4,128)S(1)} %copy.179), channel_id=1, source_target_pairs={{4,0},{8,4},{12,8},{5,1},{9,5},{13,9},{6,2},{10,6},{14,10},{7,3},{... | collective-permute-start | bytes 10376 | tf_op jit(solution)/shard_map/ppermute | solution.py:25
  58.9 2.9 %collective-permute-start.8 = (f32[3,1,3,32]{3,0,2,1:T(4,128)S(1)}, f32[3,1,3,32]{3,0,2,1:T(4,128)S(1)}, u32[]{:S(2)}, u32[]{:S(2)}) collective-permute-start(f32[3,1,3,32]{3,0,2,1:T(4,128)S(1)} %get-tuple-element.29), channel_id=1, source_target_pairs={{0,2},{1,3},{4,6},{5,7},{8,10},{9,11},{12,14},{13,15},{16,18},{17,... | collective-permute-start | bytes 3464 | tf_op jit(solution)/shard_map/ppermute | solution.py:22
  60.5 5.5 %collective-permute-start.9 = (f32[3,1,3,32]{3,0,2,1:T(4,128)S(1)}, f32[3,1,3,32]{3,0,2,1:T(4,128)S(1)}, u32[]{:S(2)}, u32[]{:S(2)}) collective-permute-start(f32[3,1,3,32]{3,0,2,1:T(4,128)S(1)} %get-tuple-element.30), channel_id=1, source_target_pairs={{2,0},{3,1},{6,4},{7,5},{10,8},{11,9},{14,12},{15,13},{18,16},{19,... | collective-permute-start | bytes 3464 | tf_op jit(solution)/shard_map/ppermute | solution.py:25
  66.0 2.6 %collective-permute-start.10 = (f32[3,1,32]{2,0,1:T(4,128)S(1)}, f32[3,1,32]{2,0,1:T(4,128)S(1)}, u32[]{:S(2)}, u32[]{:S(2)}) collective-permute-start(f32[3,1,32]{2,0,1:T(4,128)S(1)} %get-tuple-element.42), channel_id=1, source_target_pairs={{0,1},{2,3},{4,5},{6,7},{8,9},{10,11},{12,13},{14,15},{16,17},{18,... | collective-permute-start | bytes 1160 | tf_op jit(solution)/shard_map/ppermute | solution.py:22
  67.3 3.1 %collective-permute-start.11 = (f32[3,1,32]{2,0,1:T(4,128)S(1)}, f32[3,1,32]{2,0,1:T(4,128)S(1)}, u32[]{:S(2)}, u32[]{:S(2)}) collective-permute-start(f32[3,1,32]{2,0,1:T(4,128)S(1)} %get-tuple-element.43), channel_id=1, source_target_pairs={{1,0},{3,2},{5,4},{7,6},{9,8},{11,10},{13,12},{15,14},{17,16},{19,... | collective-permute-start | bytes 1160 | tf_op jit(solution)/shard_map/ppermute | solution.py:25
  68.6 1.7 copy-start.9
  70.4 6.3 %collective-permute-start.12 = (f32[84,1,1,1,32]{4,0,3,2,1:T(8,128)S(1)}, f32[84,1,1,1,32]{4,0,3,2,1:T(8,128)S(1)}, u32[]{:S(2)}, u32[]{:S(2)}) collective-permute-start(f32[84,1,1,1,32]{4,0,3,2,1:T(8,128)S(1)} %fusion.24), channel_id=1, source_target_pairs={{0,4},{4,8},{8,12},{1,5},{5,9},{9,13},{2,6},{6,10},{10,14},{3,7},{... | collective-permute-start | bytes 32264 | tf_op jit(solution)/shard_map/ppermute | solution.py:22
  75.0 5.9 %collective-permute-start.13 = (f32[84,1,1,1,32]{4,0,3,2,1:T(8,128)S(1)}, f32[84,1,1,1,32]{4,0,3,2,1:T(8,128)S(1)}, u32[]{:S(2)}, u32[]{:S(2)}) collective-permute-start(f32[84,1,1,1,32]{4,0,3,2,1:T(8,128)S(1)} %fusion.24), channel_id=1, source_target_pairs={{4,0},{8,4},{12,8},{5,1},{9,5},{13,9},{6,2},{10,6},{14,10},{7,3},{... | collective-permute-start | bytes 32264 | tf_op jit(solution)/shard_map/ppermute | solution.py:25
  81.0 3.4 %collective-permute-start.14 = (f32[84,3,1,1,32]{0,4,3,2,1:T(8,128)S(1)}, f32[84,3,1,1,32]{0,4,3,2,1:T(8,128)S(1)}, u32[]{:S(2)}, u32[]{:S(2)}) collective-permute-start(f32[84,3,1,1,32]{0,4,3,2,1:T(8,128)S(1)} %pad_maximum_fusion.12), channel_id=1, source_target_pairs={{0,2},{1,3},{4,6},{5,7},{8,10},{9,11},{12,14},{13,15},{16,18},{17,... | collective-permute-start | bytes 96776 | tf_op jit(solution)/shard_map/ppermute | solution.py:22
  82.7 6.0 %collective-permute-start.15 = (f32[84,3,1,1,32]{0,4,3,2,1:T(8,128)S(1)}, f32[84,3,1,1,32]{0,4,3,2,1:T(8,128)S(1)}, u32[]{:S(2)}, u32[]{:S(2)}) collective-permute-start(f32[84,3,1,1,32]{0,4,3,2,1:T(8,128)S(1)} %pad_maximum_fusion.12), channel_id=1, source_target_pairs={{2,0},{3,1},{6,4},{7,5},{10,8},{11,9},{14,12},{15,13},{18,16},{19,... | collective-permute-start | bytes 96776 | tf_op jit(solution)/shard_map/ppermute | solution.py:25
  88.7 2.7 %collective-permute-start.16 = (f32[84,3,3,1,32]{0,4,3,2,1:T(8,128)S(1)}, f32[84,3,3,1,32]{0,4,3,2,1:T(8,128)S(1)}, u32[]{:S(2)}, u32[]{:S(2)}) collective-permute-start(f32[84,3,3,1,32]{0,4,3,2,1:T(8,128)S(1)} %pad_maximum_fusion.7), channel_id=1, source_target_pairs={{0,1},{2,3},{4,5},{6,7},{8,9},{10,11},{12,13},{14,15},{16,17},{18,... | collective-permute-start | bytes 290312 | tf_op jit(solution)/shard_map/ppermute | solution.py:22
  90.0 3.3 %collective-permute-start.17 = (f32[84,3,3,1,32]{0,4,3,2,1:T(8,128)S(1)}, f32[84,3,3,1,32]{0,4,3,2,1:T(8,128)S(1)}, u32[]{:S(2)}, u32[]{:S(2)}) collective-permute-start(f32[84,3,3,1,32]{0,4,3,2,1:T(8,128)S(1)} %pad_maximum_fusion.7), channel_id=1, source_target_pairs={{1,0},{3,2},{5,4},{7,6},{9,8},{11,10},{13,12},{15,14},{17,16},{19,... | collective-permute-start | bytes 290312 | tf_op jit(solution)/shard_map/ppermute | solution.py:25
  113.1 10.9 %collective-permute-start.18 = (f32[3,1,3,3,32]{4,0,3,2,1:T(4,128)S(1)}, f32[3,1,3,3,32]{4,0,3,2,1:T(4,128)S(1)}, u32[]{:S(2)}, u32[]{:S(2)}) collective-permute-start(f32[3,1,3,3,32]{4,0,3,2,1:T(4,128)S(1)} %copy.180), channel_id=1, source_target_pairs={{0,4},{4,8},{8,12},{1,5},{5,9},{9,13},{2,6},{6,10},{10,14},{3,7},{... | collective-permute-start | bytes 10376 | tf_op jit(solution)/shard_map/ppermute | solution.py:22
  116.7 7.4 %collective-permute-start.19 = (f32[3,1,3,3,32]{4,0,3,2,1:T(4,128)S(1)}, f32[3,1,3,3,32]{4,0,3,2,1:T(4,128)S(1)}, u32[]{:S(2)}, u32[]{:S(2)}) collective-permute-start(f32[3,1,3,3,32]{4,0,3,2,1:T(4,128)S(1)} %copy.182), channel_id=1, source_target_pairs={{4,0},{8,4},{12,8},{5,1},{9,5},{13,9},{6,2},{10,6},{14,10},{7,3},{... | collective-permute-start | bytes 10376 | tf_op jit(solution)/shard_map/ppermute | solution.py:25
  124.1 2.9 %collective-permute-start.20 = (f32[3,1,3,32]{3,0,2,1:T(4,128)S(1)}, f32[3,1,3,32]{3,0,2,1:T(4,128)S(1)}, u32[]{:S(2)}, u32[]{:S(2)}) collective-permute-start(f32[3,1,3,32]{3,0,2,1:T(4,128)S(1)} %get-tuple-element.27), channel_id=1, source_target_pairs={{0,2},{1,3},{4,6},{5,7},{8,10},{9,11},{12,14},{13,15},{16,18},{17,... | collective-permute-start | bytes 3464 | tf_op jit(solution)/shard_map/ppermute | solution.py:22
  125.7 5.5 %collective-permute-start.21 = (f32[3,1,3,32]{3,0,2,1:T(4,128)S(1)}, f32[3,1,3,32]{3,0,2,1:T(4,128)S(1)}, u32[]{:S(2)}, u32[]{:S(2)}) collective-permute-start(f32[3,1,3,32]{3,0,2,1:T(4,128)S(1)} %get-tuple-element.28), channel_id=1, source_target_pairs={{2,0},{3,1},{6,4},{7,5},{10,8},{11,9},{14,12},{15,13},{18,16},{19,... | collective-permute-start | bytes 3464 | tf_op jit(solution)/shard_map/ppermute | solution.py:25
  131.2 2.6 %collective-permute-start.22 = (f32[3,1,32]{2,0,1:T(4,128)S(1)}, f32[3,1,32]{2,0,1:T(4,128)S(1)}, u32[]{:S(2)}, u32[]{:S(2)}) collective-permute-start(f32[3,1,32]{2,0,1:T(4,128)S(1)} %get-tuple-element.40), channel_id=1, source_target_pairs={{0,1},{2,3},{4,5},{6,7},{8,9},{10,11},{12,13},{14,15},{16,17},{18,... | collective-permute-start | bytes 1160 | tf_op jit(solution)/shard_map/ppermute | solution.py:22
  132.5 3.1 %collective-permute-start.23 = (f32[3,1,32]{2,0,1:T(4,128)S(1)}, f32[3,1,32]{2,0,1:T(4,128)S(1)}, u32[]{:S(2)}, u32[]{:S(2)}) collective-permute-start(f32[3,1,32]{2,0,1:T(4,128)S(1)} %get-tuple-element.41), channel_id=1, source_target_pairs={{1,0},{3,2},{5,4},{7,6},{9,8},{11,10},{13,12},{15,14},{17,16},{19,... | collective-permute-start | bytes 1160 | tf_op jit(solution)/shard_map/ppermute | solution.py:25
  135.7 6.3 %collective-permute-start.24 = (f32[84,1,1,1,32]{4,0,3,2,1:T(8,128)S(1)}, f32[84,1,1,1,32]{4,0,3,2,1:T(8,128)S(1)}, u32[]{:S(2)}, u32[]{:S(2)}) collective-permute-start(f32[84,1,1,1,32]{4,0,3,2,1:T(8,128)S(1)} %fusion.22), channel_id=1, source_target_pairs={{0,4},{4,8},{8,12},{1,5},{5,9},{9,13},{2,6},{6,10},{10,14},{3,7},{... | collective-permute-start | bytes 32264 | tf_op jit(solution)/shard_map/ppermute | solution.py:22
  140.2 5.9 %collective-permute-start.25 = (f32[84,1,1,1,32]{4,0,3,2,1:T(8,128)S(1)}, f32[84,1,1,1,32]{4,0,3,2,1:T(8,128)S(1)}, u32[]{:S(2)}, u32[]{:S(2)}) collective-permute-start(f32[84,1,1,1,32]{4,0,3,2,1:T(8,128)S(1)} %fusion.22), channel_id=1, source_target_pairs={{4,0},{8,4},{12,8},{5,1},{9,5},{13,9},{6,2},{10,6},{14,10},{7,3},{... | collective-permute-start | bytes 32264 | tf_op jit(solution)/shard_map/ppermute | solution.py:25
  146.2 3.4 %collective-permute-start.26 = (f32[84,3,1,1,32]{0,4,3,2,1:T(8,128)S(1)}, f32[84,3,1,1,32]{0,4,3,2,1:T(8,128)S(1)}, u32[]{:S(2)}, u32[]{:S(2)}) collective-permute-start(f32[84,3,1,1,32]{0,4,3,2,1:T(8,128)S(1)} %pad_maximum_fusion.13), channel_id=1, source_target_pairs={{0,2},{1,3},{4,6},{5,7},{8,10},{9,11},{12,14},{13,15},{16,18},{17,... | collective-permute-start | bytes 96776 | tf_op jit(solution)/shard_map/ppermute | solution.py:22
  147.9 6.0 %collective-permute-start.27 = (f32[84,3,1,1,32]{0,4,3,2,1:T(8,128)S(1)}, f32[84,3,1,1,32]{0,4,3,2,1:T(8,128)S(1)}, u32[]{:S(2)}, u32[]{:S(2)}) collective-permute-start(f32[84,3,1,1,32]{0,4,3,2,1:T(8,128)S(1)} %pad_maximum_fusion.13), channel_id=1, source_target_pairs={{2,0},{3,1},{6,4},{7,5},{10,8},{11,9},{14,12},{15,13},{18,16},{19,... | collective-permute-start | bytes 96776 | tf_op jit(solution)/shard_map/ppermute | solution.py:25
  153.9 2.7 %collective-permute-start.28 = (f32[84,3,3,1,32]{0,4,3,2,1:T(8,128)S(1)}, f32[84,3,3,1,32]{0,4,3,2,1:T(8,128)S(1)}, u32[]{:S(2)}, u32[]{:S(2)}) collective-permute-start(f32[84,3,3,1,32]{0,4,3,2,1:T(8,128)S(1)} %pad_maximum_fusion.8), channel_id=1, source_target_pairs={{0,1},{2,3},{4,5},{6,7},{8,9},{10,11},{12,13},{14,15},{16,17},{18,... | collective-permute-start | bytes 290312 | tf_op jit(solution)/shard_map/ppermute | solution.py:22
  155.2 3.3 %collective-permute-start.29 = (f32[84,3,3,1,32]{0,4,3,2,1:T(8,128)S(1)}, f32[84,3,3,1,32]{0,4,3,2,1:T(8,128)S(1)}, u32[]{:S(2)}, u32[]{:S(2)}) collective-permute-start(f32[84,3,3,1,32]{0,4,3,2,1:T(8,128)S(1)} %pad_maximum_fusion.8), channel_id=1, source_target_pairs={{1,0},{3,2},{5,4},{7,6},{9,8},{11,10},{13,12},{15,14},{17,16},{19,... | collective-permute-start | bytes 290312 | tf_op jit(solution)/shard_map/ppermute | solution.py:25
  178.4 10.9 %collective-permute-start.30 = (f32[3,1,3,3,32]{4,0,3,2,1:T(4,128)S(1)}, f32[3,1,3,3,32]{4,0,3,2,1:T(4,128)S(1)}, u32[]{:S(2)}, u32[]{:S(2)}) collective-permute-start(f32[3,1,3,3,32]{4,0,3,2,1:T(4,128)S(1)} %copy.183), channel_id=1, source_target_pairs={{0,4},{4,8},{8,12},{1,5},{5,9},{9,13},{2,6},{6,10},{10,14},{3,7},{... | collective-permute-start | bytes 10376 | tf_op jit(solution)/shard_map/ppermute | solution.py:22
  181.9 7.4 %collective-permute-start.31 = (f32[3,1,3,3,32]{4,0,3,2,1:T(4,128)S(1)}, f32[3,1,3,3,32]{4,0,3,2,1:T(4,128)S(1)}, u32[]{:S(2)}, u32[]{:S(2)}) collective-permute-start(f32[3,1,3,3,32]{4,0,3,2,1:T(4,128)S(1)} %copy.185), channel_id=1, source_target_pairs={{4,0},{8,4},{12,8},{5,1},{9,5},{13,9},{6,2},{10,6},{14,10},{7,3},{... | collective-permute-start | bytes 10376 | tf_op jit(solution)/shard_map/ppermute | solution.py:25
  189.3 2.9 %collective-permute-start.32 = (f32[3,1,3,32]{3,0,2,1:T(4,128)S(1)}, f32[3,1,3,32]{3,0,2,1:T(4,128)S(1)}, u32[]{:S(2)}, u32[]{:S(2)}) collective-permute-start(f32[3,1,3,32]{3,0,2,1:T(4,128)S(1)} %get-tuple-element.25), channel_id=1, source_target_pairs={{0,2},{1,3},{4,6},{5,7},{8,10},{9,11},{12,14},{13,15},{16,18},{17,... | collective-permute-start | bytes 3464 | tf_op jit(solution)/shard_map/ppermute | solution.py:22
  190.9 5.5 %collective-permute-start.33 = (f32[3,1,3,32]{3,0,2,1:T(4,128)S(1)}, f32[3,1,3,32]{3,0,2,1:T(4,128)S(1)}, u32[]{:S(2)}, u32[]{:S(2)}) collective-permute-start(f32[3,1,3,32]{3,0,2,1:T(4,128)S(1)} %get-tuple-element.26), channel_id=1, source_target_pairs={{2,0},{3,1},{6,4},{7,5},{10,8},{11,9},{14,12},{15,13},{18,16},{19,... | collective-permute-start | bytes 3464 | tf_op jit(solution)/shard_map/ppermute | solution.py:25
  196.4 3.3 %collective-permute-start.34 = (f32[3,1,32]{2,0,1:T(4,128)S(1)}, f32[3,1,32]{2,0,1:T(4,128)S(1)}, u32[]{:S(2)}, u32[]{:S(2)}) collective-permute-start(f32[3,1,32]{2,0,1:T(4,128)S(1)} %get-tuple-element.38), channel_id=1, source_target_pairs={{0,1},{2,3},{4,5},{6,7},{8,9},{10,11},{12,13},{14,15},{16,17},{18,... | collective-permute-start | bytes 1160 | tf_op jit(solution)/shard_map/ppermute | solution.py:22
  197.7 3.1 %collective-permute-start.35 = (f32[3,1,32]{2,0,1:T(4,128)S(1)}, f32[3,1,32]{2,0,1:T(4,128)S(1)}, u32[]{:S(2)}, u32[]{:S(2)}) collective-permute-start(f32[3,1,32]{2,0,1:T(4,128)S(1)} %get-tuple-element.39), channel_id=1, source_target_pairs={{1,0},{3,2},{5,4},{7,6},{9,8},{11,10},{13,12},{15,14},{17,16},{19,... | collective-permute-start | bytes 1160 | tf_op jit(solution)/shard_map/ppermute | solution.py:25
  (5 other events, 3.5 us)
where the time goes:
time: 203 us; the launch traced here: 201 us
  starting transfers between devices  68.3 us (34%)
  waiting for transfers between devices  45.6 us (22%)
  local copies, waits for them, and re-layouts  42.3 us (21%)
  other arithmetic  40.2 us (20%)
  matrix products  2.59 us (1%)
  between operations  2.48 us (1%)
    ppermute x18, starting transfers between devices, extended_2(): lax.ppermute(lax.slice_in_dim(block, block.shape[dim] - width, None, axis...  44.9 us
    ppermute x18, waiting for transfers between devices, extended_2(): lax.ppermute(lax.slice_in_dim(block, 0, width, axis=dim), axis, backward)  43.8 us
    scatter-add x3, other arithmetic, domain_update(): jax.ops.segment_sum(flat_field, cosmo_index.reshape(-1), num_segments=can...  34.7 us
    ppermute x18, starting transfers between devices, extended_2(): lax.ppermute(lax.slice_in_dim(block, 0, width, axis=dim), axis, backward)  23.4 us
    gather x6, local copies, waits for them, and re-layouts, domain_update(): partner = jnp.take(candidates[coef_count:], thole_index, axis=1)  17.4 us
    gather x3, local copies, waits for them, and re-layouts, domain_update(): neighbours = jnp.take(candidates[:coef_count], cosmo_index, axis=1)  16.4 us
    unnamed x44, local copies, waits for them, and re-layouts  5.26 us
  transfers between devices with their start and end apart: 36, of which 19 were waited for; matrix products, arithmetic and copies ran while one was open for 10% of the time, Pallas kernels for 0%

commit v1 on v0

v1 whole, which is shorter than its diff:
```python
import functools
import itertools
import math

import jax
import jax.numpy as jnp
from jax import lax
from jax.experimental import pallas as pl
from jax.experimental.pallas import tpu as pltpu
from jax.sharding import PartitionSpec as P

ITERS = 3
AXES = ("gx", "gy", "gz")
MESH = pl.DeviceIdType.MESH
THOLE_DAMPING = 0.39
INJECT_SCALE = 2.0
RADIUS_SCALE = 0.9

COEF = 81
GRID = 302
LANES = 128
BORDER = 32
PAIRS = 16
GROUPS = LANES // BORDER
PACK = 24
ROWS = GROUPS * PACK
CROWS = 88
GRID_PAD = 304
GRID_K = 384
F32 = jnp.float32
BF16 = jnp.bfloat16


def axis_digits(size):
    if size >= 3:
        return (-1, 0, 1)
    return (0, 1) if size == 2 else (0,)


class Slots:
    def __init__(self, sizes):
        self.sizes = sizes
        self.digits = [axis_digits(n) for n in sizes]
        self.all = list(itertools.product(*[range(len(d)) for d in self.digits]))
        self.count = len(self.all)
        self.tiles = -(-self.count // GROUPS)
        centre = tuple(d.index(0) for d in self.digits)
        self.own = self.all.index(centre)
        self.others = [i for i in range(self.count) if i != self.own]

    def mirror(self, slot):
        place = self.all[slot]
        back = tuple(2 - e if n >= 3 else e for e, n in zip(place, self.sizes))
        return self.all.index(back)

    def device(self, slot, me):
        ids = {}
        for axis, n, d, e, i in zip(AXES, self.sizes, self.digits, self.all[slot], me):
            if d[e] == 0:
                continue
            ids[axis] = i + d[e] if n >= 3 else 1 - i
        return ids

    def valid(self, slot, me):
        cond = None
        for n, d, e, i in zip(self.sizes, self.digits, self.all[slot], me):
            if n < 3 or d[e] == 0:
                continue
            here = (i + d[e] >= 0) & (i + d[e] < n)
            cond = here if cond is None else cond & here
        return cond


def when(cond, fn):
    if cond is None:
        fn()
    else:
        pl.when(cond)(fn)


def lane_group(shape):
    return lax.broadcasted_iota(jnp.int32, shape, len(shape) - 1) >> 5


def lane_take(table, lanes):
    return jnp.take_along_axis(table, lanes, axis=1, mode="promise_in_bounds")


def rolled(x, shift):
    shift = shift % LANES
    return x if shift == 0 else pltpu.roll(x, shift, 1)


def degree_rows(rows):
    row = lax.broadcasted_iota(jnp.int32, (rows, LANES), 0)
    total = jnp.zeros((rows, LANES), F32)
    for level in range(1, math.isqrt(COEF)):
        total = total + jnp.where(row >= level * level, 1.0, 0.0)
    return total


def split(x):
    high = x.astype(BF16)
    return high, (x - high.astype(F32)).astype(BF16)


def columns(index, me, plan):
    block = index >> 5
    within = index & 31
    bx = (block * 57) >> 9
    rest = block - 9 * bx
    by = (rest * 171) >> 9
    bz = rest - 3 * by
    inside = None
    slot = jnp.zeros_like(index)
    for n, d, b, i in zip(plan.sizes, plan.digits, (bx, by, bz), me):
        step = b - 1
        here = (step + i >= 0) & (step + i < n)
        inside = here if inside is None else inside & here
        digit = b if n >= 3 else step * step
        slot = slot * len(d) + (digit if n >= 2 else jnp.zeros_like(index))
    remote = jnp.where(inside, LANES + slot * BORDER + within, -1)
    column = jnp.where(block == 13, within, remote)
    return jnp.where(index >= 27 * BORDER, index - 27 * BORDER, column)


def kernel(
    plan,
    coef_ref, dip_ref, source_ref, ind_ref, polar_ref, ext_ref, counts_ref,
    cidx_ref, cw_ref, cd_ref, ct_ref, cp_ref,
    tidx_ref, tw_ref, td_ref, tt_ref, tp_ref,
    harm_ref, leb_ref,
    coef_out, dip_out,
    cs, ds, src, inj, ext, tmp, sbuf, cbuf, fdbuf, fdrecv,
    colb, pk, wr, wrp, edir, edirp, stren, ohown, ohrem, fown, frem,
    hk, ht, htm, hsq, zs, ws, ind, thc, pool,
    csend, crecv, fsend, frecv,
):
    me = tuple(lax.axis_index(a) for a in AXES)
    group24 = lane_group((PACK, LANES))
    group8 = lane_group((8, LANES))
    iota8 = lax.broadcasted_iota(jnp.int32, (8, LANES), 0)

    cs[...] = jnp.zeros_like(cs)
    ds[...] = jnp.zeros_like(ds)
    cs[0:COEF, :] = coef_ref[...]
    ds[0:3, :] = dip_ref[...]
    for slot in plan.others:
        cond = plan.valid(slot, me)
        if cond is not None:
            def clear(slot=slot):
                for s in range(ITERS):
                    cbuf[s, slot] = jnp.zeros((PACK, LANES), F32)
                    fdrecv[s, slot] = jnp.zeros((8, LANES), F32)
            pl.when(jnp.logical_not(cond))(clear)

    barrier = pltpu.get_barrier_semaphore()
    number = 0
    for slot in plan.others:
        cond = plan.valid(slot, me)
        ids = plan.device(slot, me)
        when(cond, lambda ids=ids: pl.semaphore_signal(barrier, inc=1, device_id=ids, device_id_type=MESH))
        number = number + (1 if cond is None else cond.astype(jnp.int32))

    def c_copy(s, slot, arriving=False):
        back = slot if arriving else plan.mirror(slot)
        return pltpu.make_async_remote_copy(
            src_ref=sbuf.at[s], dst_ref=cbuf.at[s, back],
            send_sem=csend.at[s, slot], recv_sem=crecv.at[s, back],
            device_id=plan.device(slot, me), device_id_type=MESH,
        )

    def f_copy(s, slot, arriving=False):
        back = slot if arriving else plan.mirror(slot)
        return pltpu.make_async_remote_copy(
            src_ref=fdbuf.at[s, slot // GROUPS], dst_ref=fdrecv.at[s, back],
            send_sem=fsend.at[s, slot], recv_sem=frecv.at[s, back],
            device_id=plan.device(slot, me), device_id_type=MESH,
        )

    def each(make, s, act):
        for slot in plan.others:
            when(plan.valid(slot, me), lambda slot=slot: act(make(s, slot)))

    def arrive(make, s):
        for slot in plan.others:
            when(plan.valid(slot, me), lambda slot=slot: make(s, slot, True).wait_recv())

    def pack_coefs(s):
        packed = cs[0:PACK, :]
        for j in range(1, GROUPS):
            packed = jnp.where(group24 == j, rolled(cs[j * PACK:(j + 1) * PACK, :], BORDER * j), packed)
        sbuf[s] = packed

    pack_coefs(0)
    pl.semaphore_wait(barrier, number)
    each(c_copy, 0, lambda c: c.start())

    zero8 = jnp.zeros((8, LANES), F32)
    src[...] = jnp.zeros_like(src)
    src[0:COEF, :] = source_ref[...]
    inj[...] = jnp.zeros_like(inj)
    ext[...] = zero8
    ext[0:3, :] = ext_ref[...]
    tmp[...] = zero8
    ind[...] = jnp.zeros_like(ind)
    ind[0:GRID, :] = ind_ref[...]
    zs[...] = jnp.zeros_like(zs)
    ws[...] = jnp.zeros_like(ws)
    hsq[...] = jnp.zeros_like(hsq)
    hsq[0:GRID, 0:COEF] = harm_ref[...]
    pk[...] = jnp.zeros_like(pk)
    colb[...] = jnp.zeros_like(colb)
    edir[...] = jnp.zeros_like(edir)
    edirp[...] = jnp.zeros_like(edirp)
    stren[...] = jnp.zeros_like(stren)

    def project_tables():
        square = hsq[...]
        high, low = split(square[0:GRID_PAD])
        hk[:, 0:LANES] = high
        hk[:, LANES:] = low
        turned = square.T[0:ROWS]
        lebedev = jnp.broadcast_to(leb_ref[...], (ROWS, GRID))
        hsq[0:ROWS, :] = jnp.zeros((ROWS, LANES), F32)
        return turned, lebedev

    turned, lebedev = project_tables()
    lebw = jnp.concatenate([lebedev, jnp.zeros((ROWS, GRID_K - GRID), F32)], axis=1)
    weighted = turned * lebw
    high, low = split(weighted)
    ht[0:ROWS, :] = high
    ht[ROWS:, :] = low
    rowk = lax.broadcasted_iota(jnp.int32, (8, GRID_K), 0)
    three = jnp.where(rowk < 3, pltpu.roll(weighted[0:8], 7, 0), 0.0)
    high3 = three.astype(BF16).astype(F32)
    htm[...] = jnp.concatenate([high3, three - high3], axis=0).astype(BF16)

    live = jnp.where(lax.broadcasted_iota(jnp.int32, (1, LANES), 1) < counts_ref[0, 0], 1.0, 0.0)
    degrees = degree_rows(ROWS)
    gain = live * (2.0 * degrees + 1.0) / (4.0 * math.pi)
    degrees = degrees[0:CROWS]

    column = columns(cidx_ref[...], me, plan)
    weight = cw_ref[...]
    dist = cd_ref[...]
    sin_t = jnp.sin(ct_ref[...])
    phi = cp_ref[...]
    colb[0:PAIRS, :] = column
    values = (
        weight,
        jnp.log(RADIUS_SCALE / dist),
        weight / (dist * dist * dist),
        sin_t * jnp.cos(phi),
        sin_t * jnp.sin(phi),
        jnp.cos(ct_ref[...]),
    )
    for v, value in enumerate(values):
        pk[v, 0:PAIRS, :] = value

    def packed_of(load):
        out = load(0)
        for j in range(1, GROUPS):
            out = jnp.where(group8 == j, rolled(load(GROUPS * j), BORDER * j), out)
        return out

    column_p = packed_of(lambda r: colb[r:r + 8, :])
    value_p = [packed_of(lambda r, v=v: pk[v, r:r + 8, :]) for v in range(len(values))]

    in_own = (column >= 0) & (column < LANES)
    weight_own = jnp.where(in_own, weight, 0.0)
    lanes_own = column & (LANES - 1)
    weight_rem = jnp.where(column_p >= LANES, value_p[0], 0.0)
    lanes_rem = column_p & (LANES - 1)
    tile_rem = column_p >> 7

    def spread(row, rows):
        return jnp.broadcast_to(row, (rows, LANES))

    row128 = lax.broadcasted_iota(jnp.int32, (LANES, LANES), 0)
    for k in range(PAIRS):
        wr[k] = jnp.exp(degrees * spread(values[1][k:k + 1], CROWS)) * spread(weight_own[k:k + 1], CROWS)
        ohown[:, k * LANES:(k + 1) * LANES] = jnp.where(row128 == spread(column[k:k + 1], LANES), 1.0, 0.0).astype(BF16)
        for c in range(3):
            edir[k, c:c + 1, :] = values[3 + c][k:k + 1]
    for g in range(GROUPS):
        wrp[g] = jnp.exp(degrees * spread(value_p[1][g:g + 1], CROWS)) * spread(weight_rem[g:g + 1], CROWS)
        for t in range(plan.tiles):
            ohrem[t * LANES:(t + 1) * LANES, g * LANES:(g + 1) * LANES] = jnp.where(
                row128 + (t + 1) * LANES == spread(column_p[g:g + 1], LANES), 1.0, 0.0
            ).astype(BF16)
        for c in range(3):
            edirp[g, c:c + 1, :] = value_p[3 + c][g:g + 1]

    tcol = columns(tidx_ref[...], me, plan)
    cubed = td_ref[...] * td_ref[...] * td_ref[...]
    screen = jnp.exp(-THOLE_DAMPING * cubed)
    scaled = tw_ref[...] / cubed
    lam3 = scaled * (1.0 - screen)
    lam5 = 3.0 * scaled * (1.0 - (1.0 + THOLE_DAMPING * cubed) * screen)
    tsin = jnp.sin(tt_ref[...])
    for v, value in enumerate((
        tsin * jnp.cos(tp_ref[...]), tsin * jnp.sin(tp_ref[...]), jnp.cos(tt_ref[...]), lam3, lam5,
    )):
        thc[v] = value
    tlanes = tcol & (LANES - 1)
    ttile = tcol >> 7

    def moment_fields(s):
        put_columns(cs[...])
        out = jnp.dot(htm[...], point_values(), preferred_element_type=F32)
        moment = out[0:8, 0:LANES] + out[0:8, LANES:] + out[8:, 0:LANES]
        packed = jnp.where(group8 == 0, moment, 0.0)
        wide = packed
        for j in range(1, GROUPS):
            wide = wide + rolled(packed, BORDER * j)

        def field(e, strength, m):
            along = jnp.sum(e * m, axis=0, keepdims=True)
            f = strength * (3.0 * e * along - m)
            high = f.astype(BF16).astype(F32)
            return jnp.concatenate([high, f - high], axis=0).astype(BF16)

        for k in range(PAIRS):
            fown[:, k * LANES:(k + 1) * LANES] = field(edir[k], values[2][k:k + 1], moment)
        for g in range(GROUPS):
            frem[:, g * LANES:(g + 1) * LANES] = field(edirp[g], value_p[2][g:g + 1], wide)
        turn = (((1,), (1,)), ((), ()))
        away = lax.dot_general(frem[...], ohrem[...], turn, preferred_element_type=F32)
        dip_rows = pltpu.roll(ds[...], 3, 0)
        for t in range(plan.tiles):
            part = away[:, t * LANES:(t + 1) * LANES]
            fdbuf[s, t] = jnp.where(iota8 < 3, part[0:8] + part[8:], dip_rows)
        each(f_copy, s, lambda c: c.start())
        mine = lax.dot_general(fown[...], ohown[...], turn, preferred_element_type=F32)
        return mine[0:8] + mine[8:]

    def put_columns(z):
        high, low = split(z)
        for base in (0, LANES):
            zs[base:base + ROWS, 0:LANES] = high
            zs[base:base + ROWS, LANES:] = low

    def point_values():
        out = jnp.dot(hk[...], zs[...], preferred_element_type=F32)
        high, low = split((out[:, 0:LANES] + out[:, LANES:]) * ind[...])
        ws[0:GRID_PAD, 0:LANES] = high
        ws[0:GRID_PAD, LANES:] = low
        return ws[...]

    for s in range(ITERS):
        own_field = moment_fields(s)

        table = cs[0:CROWS, :]
        coupled = jnp.zeros((CROWS, LANES), F32)
        for k in range(PAIRS):
            coupled = coupled + wr[k] * lane_take(table, spread(lanes_own[k:k + 1], CROWS))
        arrive(c_copy, s)
        for t in range(plan.tiles):
            for j in range(GROUPS):
                block = jnp.zeros((PACK, LANES), F32)
                for m in range(GROUPS):
                    slot = GROUPS * t + m
                    if slot >= plan.count or slot == plan.own:
                        continue
                    block = jnp.where(group24 == m, rolled(cbuf[s, slot], BORDER * (m - j)), block)
                pool[t, j * PACK:(j + 1) * PACK, :] = block
        far = jnp.zeros((CROWS, LANES), F32)
        for g in range(GROUPS):
            lanes = spread(lanes_rem[g:g + 1], CROWS)
            tiles = spread(tile_rem[g:g + 1], CROWS)
            got = lane_take(pool[0, 0:CROWS, :], lanes)
            for t in range(1, plan.tiles):
                got = jnp.where(tiles == t + 1, lane_take(pool[t, 0:CROWS, :], lanes), got)
            far = far + wrp[g] * got
        far = far + rolled(far, 64)
        far = far + rolled(far, 32)
        coupled = coupled + jnp.where(lane_group((CROWS, LANES)) == 0, far, 0.0)

        put_columns(jnp.concatenate([coupled, zero8], axis=0))
        inj[1:4, :] = INJECT_SCALE * ds[0:3, :]
        out = jnp.dot(ht[...], point_values(), preferred_element_type=F32)
        projected = out[0:ROWS, 0:LANES] + out[0:ROWS, LANES:] + out[ROWS:, 0:LANES]
        fresh = gain * (src[...] + inj[...] - projected)
        if s < ITERS - 1:
            cs[...] = fresh
            pack_coefs(s + 1)
            each(c_copy, s + 1, lambda c: c.start())
        else:
            coef_out[...] = fresh[0:COEF]

        arrive(f_copy, s)
        reaction = own_field
        for m in range(GROUPS):
            total = None
            for slot in plan.others:
                if plan.mirror(slot) % GROUPS == m:
                    total = fdrecv[s, slot] if total is None else total + fdrecv[s, slot]
            if total is not None:
                reaction = reaction + jnp.where(group8 == 0, rolled(total, -BORDER * m), 0.0)
        tables = [pltpu.roll(ds[...], 3, 0)]
        for t in range(plan.tiles):
            block = zero8
            for m in range(GROUPS):
                slot = GROUPS * t + m
                if slot >= plan.count or slot == plan.own:
                    continue
                block = jnp.where(group8 == m, rolled(fdrecv[s, slot], BORDER * m), block)
            tables.append(block)
        partner = []
        for c in range(3):
            got = jnp.zeros((PAIRS, LANES), F32)
            for t, block in enumerate(tables):
                got = jnp.where(ttile == t, lane_take(spread(block[3 + c:4 + c], PAIRS), tlanes), got)
            partner.append(got)
        along = thc[4] * (thc[0] * partner[0] + thc[1] * partner[1] + thc[2] * partner[2])
        for c in range(3):
            tmp[c:c + 1, :] = jnp.sum(thc[c] * along - thc[3] * partner[c], axis=0, keepdims=True)
        moved = live * polar_ref[...] * (ext[...] + tmp[...] + reaction)
        moved = jnp.where(iota8 < 3, moved, 0.0)
        if s < ITERS - 1:
            ds[...] = moved
        else:
            dip_out[...] = moved[0:3]

    for s in range(ITERS):
        each(c_copy, s, lambda c: c.wait_send())
        each(f_copy, s, lambda c: c.wait_send())


def rows_of(x):
    return x.reshape(x.shape[0], x.shape[-1])


def local(plan, *args):
    (coef, dip, source, ind, polar, ext, counts, cidx, cw, cd, ct, cp,
     tidx, tw, td, tt, tp, harm, leb) = args
    flat = [rows_of(x) for x in (coef, dip, source, ind)]
    flat += [polar.reshape(1, LANES), rows_of(ext), counts.reshape(1, 1)]
    flat += [rows_of(x) for x in (cidx, cw, cd, ct, cp, tidx, tw, td, tt, tp)]
    flat += [harm, leb.reshape(1, GRID)]
    vmem = pl.BlockSpec(memory_space=pltpu.VMEM)
    smem = pl.BlockSpec(memory_space=pltpu.SMEM)
    scratch = [
        ((ROWS, LANES), F32), ((8, LANES), F32), ((ROWS, LANES), F32), ((ROWS, LANES), F32),
        ((8, LANES), F32), ((8, LANES), F32),
        ((ITERS, PACK, LANES), F32), ((ITERS, plan.count, PACK, LANES), F32),
        ((ITERS, plan.tiles, 8, LANES), F32), ((ITERS, plan.count, 8, LANES), F32),
        ((24, LANES), jnp.int32), ((6, 24, LANES), F32),
        ((PAIRS, CROWS, LANES), F32), ((GROUPS, CROWS, LANES), F32),
        ((PAIRS, 8, LANES), F32), ((GROUPS, 8, LANES), F32), ((8, LANES), F32),
        ((LANES, PAIRS * LANES), BF16), ((plan.tiles * LANES, GROUPS * LANES), BF16),
        ((16, PAIRS * LANES), BF16), ((16, GROUPS * LANES), BF16),
        ((GRID_PAD, 2 * LANES), BF16), ((2 * ROWS, GRID_K), BF16), ((16, GRID_K), BF16),
        ((GRID_K, LANES), F32),
        ((2 * LANES, 2 * LANES), BF16), ((GRID_K, 2 * LANES), BF16), ((GRID_PAD, LANES), F32),
        ((5, PAIRS, LANES), F32), ((plan.tiles, ROWS, LANES), F32),
    ]
    semaphores = [pltpu.SemaphoreType.DMA((ITERS, plan.count))] * 4
    coef_new, dip_new = pl.pallas_call(
        functools.partial(kernel, plan),
        out_shape=(jax.ShapeDtypeStruct((COEF, LANES), F32), jax.ShapeDtypeStruct((3, LANES), F32)),
        in_specs=[smem if i == 6 else vmem for i in range(len(flat))],
        out_specs=(vmem, vmem),
        scratch_shapes=[pltpu.VMEM(shape, kind) for shape, kind in scratch] + semaphores,
        compiler_params=pltpu.CompilerParams(
            collective_id=0, has_side_effects=True, vmem_limit_bytes=32 * 1024 * 1024
        ),
    )(*flat)
    return coef_new.reshape(coef.shape), dip_new.reshape(dip.shape)


def solution(mesh):
    plan = Slots(tuple(mesh.shape[a] for a in AXES))
    lead = P(None, ("grp", "gx"), "gy", "gz", None)
    flat = P(("grp", "gx"), "gy", "gz", None)
    in_specs = (lead,) * 4 + (flat, lead, P(("grp", "gx"), "gy", "gz")) + (lead,) * 10 + (P(), P())
    return jax.shard_map(
        functools.partial(local, plan), mesh=mesh, in_specs=in_specs, out_specs=(lead, lead), check_vma=False
    )
```

time: 203 us -> 27.3 us (0.13)
  starting transfers between devices: 68.3 us -> 0 us
  waiting for transfers between devices: 45.6 us -> 0 us
  other arithmetic: 40.2 us -> 0 us
  local copies, waits for them, and re-layouts: 42.3 us -> 5.09 us
  Pallas kernels: 0 us -> 20.5 us
  matrix products: 2.59 us -> 0 us
    ppermute x36 -> x0, starting transfers between devices: 68.3 us -> none  [the longest x18 44.9 us: extended_2(): lax.ppermute(lax.slice_in_dim(block, block.shape[dim] - width, None, axis...]
    ppermute x36 -> x0, waiting for transfers between devices: 45.6 us -> none  [the longest x18 43.8 us: extended_2(): lax.ppermute(lax.slice_in_dim(block, 0, width, axis=dim), axis, backward)]
    scatter-add x3 -> x0, other arithmetic: 34.7 us -> none  [domain_update(): jax.ops.segment_sum(flat_field, cosmo_index.reshape(-1), num_segments=can...]
    gather x9 -> x0, local copies, waits for them, and re-layouts: 33.8 us -> none  [the longest x6 17.4 us: domain_update(): partner = jnp.take(candidates[coef_count:], thole_index, axis=1)]
    pallas_call x0 -> x1, Pallas kernels: none -> 20.5 us  [local(): pl.pallas_call(functools.partial(kernel, plan), out_shape=(jax.ShapeDtype...]
    reduce_sum x13 -> x0, other arithmetic: 3.17 us -> none  [the longest x3 2.93 us: domain_update(): coupled = jnp.sum(cosmo_weight[None] * radial * neighbours, axis=1)]
    dot_general x6 -> x0, matrix products: 2.59 us -> none  [the longest x3 1.48 us: domain_update(): jnp.dot(harmonics, stacked, precision=PRECISE, preferred_element_type=jnp...]
    unnamed x44 -> x32, local copies, waits for them, and re-layouts: 5.26 us -> 4.4 us
  transfers between devices with their start and end apart: 36 -> 0, of which waited for: 19 -> 0; matrix products, arithmetic and copies ran while one was open for 10% -> 0% of each run, Pallas kernels for 0% -> 0%
where the time goes in v1:
time: 27.3 us; the launch traced here: 27 us
  Pallas kernels  20.5 us (75%)
  local copies, waits for them, and re-layouts  5.09 us (19%)
  between operations  1.42 us (5%)
    pallas_call x1, Pallas kernels, local(): pl.pallas_call(functools.partial(kernel, plan), out_shape=(jax.ShapeDtype...  20.5 us
    unnamed x32, local copies, waits for them, and re-layouts  4.4 us
    reshape x1, local copies, waits for them, and re-layouts, local(): flat += [harm, leb.reshape(1, GRID)]  0.68 us

profile of v1, /device:TPU:0, one launch (start us, length us, event | category | flops | bytes accessed | tf_op | source)
XLA Modules:
  0.0 27.0 jit_solution(14840181804759813813)
XLA Ops:
  0.6 0.0 copy-start.11
  1.3 0.7 %reshape.81.leb_ref = f32[1,302]{1,0:T(1,128)S(1)} reshape(f32[302]{0:T(512)} %param.37) | data formatting | bytes 2416 | tf_op jit(solution)/shard_map/reshape | solution.py:441
  2.0 0.7 %copy_bitcast_fusion.3 = (f32[3,128]{1,0:T(4,128)S(1)}, f32[3,128]{1,0:T(4,128)S(1)}) fusion(f32[3,1,1,1,128]{4,3,2,1,0:T(1,128)} %param.24, f32[3,1,1,1,128]{4,3,2,1,0:T(1,128)} %param.20), kind=kLoop, calls=%fused_computation.3 | loop fusion | bytes 6144
  2.7 0.8 %copy_bitcast_fusion.1 = (f32[81,128]{1,0:T(8,128)S(1)}, f32[81,128]{1,0:T(8,128)S(1)}) fusion(f32[81,1,1,1,128]{4,3,2,1,0:T(1,128)} %param.21, f32[81,1,1,1,128]{4,3,2,1,0:T(1,128)} %param.19), kind=kLoop, calls=%fused_computation.1 | loop fusion | bytes 165888
  3.5 0.0 copy-done.11
  3.5 0.0 copy-start.12
  3.5 0.9 %copy-done.12 = f32[302,81]{0,1:T(8,128)S(1)} copy-done((f32[302,81]{0,1:T(8,128)S(1)}, f32[302,81]{0,1:T(8,128)}, u32[]{:S(2)}) %copy-start.12) | copy-done | bytes 97872
  4.4 0.0 copy-start
  4.4 0.0 copy-start.1
  4.4 0.0 copy-start.2
  4.4 0.0 copy-start.3
  4.4 0.0 copy-start.4
  4.5 0.0 copy-start.5
  4.5 0.0 copy-start.6
  4.5 0.0 copy-start.7
  4.5 0.0 copy-start.8
  4.5 0.0 copy-start.9
  4.5 0.0 copy-start.10
  4.5 0.1 copy.21.harm_ref
  4.6 0.5 %copy-done = s32[16,1,1,1,128]{4,3,2,1,0:T(1,128)S(1)} copy-done((s32[16,1,1,1,128]{4,3,2,1,0:T(1,128)S(1)}, s32[16,1,1,1,128]{4,3,2,1,0:T(1,128)}, u32[]{:S(2)}) %copy-start) | copy-done | bytes 8216
  5.1 0.0 copy-done.1
  5.1 0.0 copy-done.2
  5.2 0.0 copy-done.3
  5.2 0.0 copy-done.4
  5.2 0.0 copy-done.5
  5.2 0.0 copy-done.6
  5.2 0.0 copy-done.7
  5.2 0.0 copy-done.8
  5.3 0.0 copy-done.9
  5.3 0.0 copy-done.10
  5.3 20.5 %shard_map.194 = (f32[81,128]{1,0:T(8,128)S(1)}, f32[3,128]{1,0:T(4,128)S(1)}) custom-call(f32[81,128]{1,0:T(8,128)S(1)} %get-tuple-element.9.coef_ref, f32[3,128]{1,0:T(4,128)S(1)} %get-tuple-element.11.dip_ref, f32[81,128]{1,0:T(8,128)S(1)} %get-tuple-element.8.source_ref, f32[302,128]{1,0:T(8,128)S(1)} %bitcast.26, f32[1,128]{1,0:T(1,128)S(1)} %bitcast.39, ...), custom_call_target="tpu_custom_call" | custom-call | tf_op jit(solution)/shard_map/pallas_call | solution.py:460
  25.8 0.7 %copy.22 = f32[81,1,1,1,128]{4,3,2,1,0:T(1,128)} copy(f32[81,1,1,1,128]{4,0,3,2,1:T(8,128)S(1)} %bitcast.27) | data formatting | bytes 82944
  26.5 0.6 %copy.23 = f32[3,1,1,1,128]{4,3,2,1,0:T(1,128)} copy(f32[3,1,1,1,128]{4,0,3,2,1:T(4,128)S(1)} %bitcast.38) | data formatting | bytes 3072
  (1 shorter events, 0.0 us)
Async XLA Ops:
  0.6 2.9 %copy-start.11 = (f32[302,1,1,1,128]{4,3,2,1,0:T(1,128)S(1)}, f32[302,1,1,1,128]{4,3,2,1,0:T(1,128)}, u32[]{:S(2)}) copy-start(f32[302,1,1,1,128]{4,3,2,1,0:T(1,128)} %param.22) | copy-start | bytes 463876
  3.5 0.9 %copy-start.12 = (f32[302,81]{0,1:T(8,128)S(1)}, f32[302,81]{0,1:T(8,128)}, u32[]{:S(2)}) copy-start(f32[302,81]{0,1:T(8,128)} %param.36) | copy-start | bytes 293548
  4.4 0.7 %copy-start = (s32[16,1,1,1,128]{4,3,2,1,0:T(1,128)S(1)}, s32[16,1,1,1,128]{4,3,2,1,0:T(1,128)}, u32[]{:S(2)}) copy-start(s32[16,1,1,1,128]{4,3,2,1,0:T(1,128)} %param.26) | copy-start | bytes 24580
  4.4 0.7 %copy-start.1 = (f32[16,1,1,1,128]{4,3,2,1,0:T(1,128)S(1)}, f32[16,1,1,1,128]{4,3,2,1,0:T(1,128)}, u32[]{:S(2)}) copy-start(f32[16,1,1,1,128]{4,3,2,1,0:T(1,128)} %param.27) | copy-start | bytes 24580
  4.4 0.7 %copy-start.2 = (f32[16,1,1,1,128]{4,3,2,1,0:T(1,128)S(1)}, f32[16,1,1,1,128]{4,3,2,1,0:T(1,128)}, u32[]{:S(2)}) copy-start(f32[16,1,1,1,128]{4,3,2,1,0:T(1,128)} %param.28) | copy-start | bytes 24580
  4.4 0.7 %copy-start.3 = (f32[16,1,1,1,128]{4,3,2,1,0:T(1,128)S(1)}, f32[16,1,1,1,128]{4,3,2,1,0:T(1,128)}, u32[]{:S(2)}) copy-start(f32[16,1,1,1,128]{4,3,2,1,0:T(1,128)} %param.29) | copy-start | bytes 24580
  4.4 0.8 %copy-start.4 = (f32[16,1,1,1,128]{4,3,2,1,0:T(1,128)S(1)}, f32[16,1,1,1,128]{4,3,2,1,0:T(1,128)}, u32[]{:S(2)}) copy-start(f32[16,1,1,1,128]{4,3,2,1,0:T(1,128)} %param.30) | copy-start | bytes 24580
  4.5 0.8 %copy-start.5 = (s32[16,1,1,1,128]{4,3,2,1,0:T(1,128)S(1)}, s32[16,1,1,1,128]{4,3,2,1,0:T(1,128)}, u32[]{:S(2)}) copy-start(s32[16,1,1,1,128]{4,3,2,1,0:T(1,128)} %param.31) | copy-start | bytes 24580
  4.5 0.8 %copy-start.6 = (f32[16,1,1,1,128]{4,3,2,1,0:T(1,128)S(1)}, f32[16,1,1,1,128]{4,3,2,1,0:T(1,128)}, u32[]{:S(2)}) copy-start(f32[16,1,1,1,128]{4,3,2,1,0:T(1,128)} %param.32) | copy-start | bytes 24580
  4.5 0.8 %copy-start.7 = (f32[16,1,1,1,128]{4,3,2,1,0:T(1,128)S(1)}, f32[16,1,1,1,128]{4,3,2,1,0:T(1,128)}, u32[]{:S(2)}) copy-start(f32[16,1,1,1,128]{4,3,2,1,0:T(1,128)} %param.33) | copy-start | bytes 24580
  4.5 0.8 %copy-start.8 = (f32[16,1,1,1,128]{4,3,2,1,0:T(1,128)S(1)}, f32[16,1,1,1,128]{4,3,2,1,0:T(1,128)}, u32[]{:S(2)}) copy-start(f32[16,1,1,1,128]{4,3,2,1,0:T(1,128)} %param.34) | copy-start | bytes 24580
  4.5 0.8 %copy-start.9 = (f32[16,1,1,1,128]{4,3,2,1,0:T(1,128)S(1)}, f32[16,1,1,1,128]{4,3,2,1,0:T(1,128)}, u32[]{:S(2)}) copy-start(f32[16,1,1,1,128]{4,3,2,1,0:T(1,128)} %param.35) | copy-start | bytes 24580
  4.5 0.8 %copy-start.10 = (f32[1,1,1,128]{3,2,1,0:T(1,128)S(1)}, f32[1,1,1,128]{3,2,1,0:T(1,128)}, u32[]{:S(2)}) copy-start(f32[1,1,1,128]{3,2,1,0:T(1,128)} %param.23) | copy-start | bytes 1540

commit v2 on v1

--- a/solution.py
+++ b/solution.py
@@ -29,6 +29,10 @@
 GRID_K = 384
 F32 = jnp.float32
 BF16 = jnp.bfloat16
+OPERANDS = (
+    "coef", "dip", "source", "ind", "cidx", "cw", "cd", "ct", "cp",
+    "tidx", "tw", "td", "tt", "tp", "ext", "polar", "harm", "leb", "counts",
+)
 
 
 def axis_digits(size):
@@ -47,6 +51,7 @@
         centre = tuple(d.index(0) for d in self.digits)
         self.own = self.all.index(centre)
         self.others = [i for i in range(self.count) if i != self.own]
+        self.others.sort(key=lambda i: -sum(a != b for a, b in zip(self.all[i][:2], centre[:2])))
 
     def mirror(self, slot):
         place = self.all[slot]
@@ -97,6 +102,19 @@
     for level in range(1, math.isqrt(COEF)):
         total = total + jnp.where(row >= level * level, 1.0, 0.0)
     return total
+
+
+def sine_cosine(angle):
+    def sine(y):
+        z = y * y
+        total = jnp.full_like(y, 1.0 / math.factorial(13))
+        for n in (11, 9, 7, 5, 3, 1):
+            total = total * z + (-1.0) ** (n // 2) / math.factorial(n)
+        return total * y
+
+    quarter = math.pi / 2 - jnp.abs(angle)
+    up = sine(math.pi / 2 - jnp.abs(quarter))
+    return jnp.where(angle < 0.0, -up, up), sine(quarter)
 
 
 def split(x):
@@ -126,25 +144,48 @@
 
 def kernel(
     plan,
-    coef_ref, dip_ref, source_ref, ind_ref, polar_ref, ext_ref, counts_ref,
-    cidx_ref, cw_ref, cd_ref, ct_ref, cp_ref,
-    tidx_ref, tw_ref, td_ref, tt_ref, tp_ref,
-    harm_ref, leb_ref,
-    coef_out, dip_out,
+    *refs,
+):
+    count = len(OPERANDS)
+    given = refs[:count]
+    coef_out, dip_out = refs[count:count + 2]
+    held = dict(zip(OPERANDS, refs[count + 2:2 * count + 2]))
+    loads = {
+        name: pltpu.make_async_copy(there, held[name], refs[-1].at[i])
+        for i, (name, there) in enumerate(zip(OPERANDS, given))
+    }
+    body(plan, loads, held, coef_out, dip_out, *refs[2 * count + 2:-1])
+
+
+def body(
+    plan, loads, held, coef_out, dip_out,
     cs, ds, src, inj, ext, tmp, sbuf, cbuf, fdbuf, fdrecv,
     colb, pk, wr, wrp, edir, edirp, stren, ohown, ohrem, fown, frem,
-    hk, ht, htm, hsq, zs, ws, ind, thc, pool,
+    hk, ht, htm, hsq, leb, zs, ws, ind, thc, pool,
     csend, crecv, fsend, frecv,
 ):
+    def got(name):
+        loads[name].wait()
+        ref = held[name]
+        return ref[:, 0, :] if len(ref.shape) == 3 else ref[...]
+
     me = tuple(lax.axis_index(a) for a in AXES)
+    barrier = pltpu.get_barrier_semaphore()
+    number = 0
+    for slot in plan.others:
+        cond = plan.valid(slot, me)
+        ids = plan.device(slot, me)
+        when(cond, lambda ids=ids: pl.semaphore_signal(barrier, inc=1, device_id=ids, device_id_type=MESH))
+        number = number + (1 if cond is None else cond.astype(jnp.int32))
+
+    for name in OPERANDS:
+        loads[name].start()
     group24 = lane_group((PACK, LANES))
     group8 = lane_group((8, LANES))
     iota8 = lax.broadcasted_iota(jnp.int32, (8, LANES), 0)
 
     cs[...] = jnp.zeros_like(cs)
     ds[...] = jnp.zeros_like(ds)
-    cs[0:COEF, :] = coef_ref[...]
-    ds[0:3, :] = dip_ref[...]
     for slot in plan.others:
         cond = plan.valid(slot, me)
         if cond is not None:
@@ -154,37 +195,28 @@
                     fdrecv[s, slot] = jnp.zeros((8, LANES), F32)
             pl.when(jnp.logical_not(cond))(clear)
 
-    barrier = pltpu.get_barrier_semaphore()
-    number = 0
-    for slot in plan.others:
-        cond = plan.valid(slot, me)
-        ids = plan.device(slot, me)
-        when(cond, lambda ids=ids: pl.semaphore_signal(barrier, inc=1, device_id=ids, device_id_type=MESH))
-        number = number + (1 if cond is None else cond.astype(jnp.int32))
-
-    def c_copy(s, slot, arriving=False):
-        back = slot if arriving else plan.mirror(slot)
+    def copy(bufs, s, slot, place):
+        src, dst, send, recv = bufs
         return pltpu.make_async_remote_copy(
-            src_ref=sbuf.at[s], dst_ref=cbuf.at[s, back],
-            send_sem=csend.at[s, slot], recv_sem=crecv.at[s, back],
+            src_ref=src(s, slot), dst_ref=dst.at[s, place],
+            send_sem=send.at[s, slot], recv_sem=recv.at[s, place],
             device_id=plan.device(slot, me), device_id_type=MESH,
         )
 
-    def f_copy(s, slot, arriving=False):
-        back = slot if arriving else plan.mirror(slot)
-        return pltpu.make_async_remote_copy(
-            src_ref=fdbuf.at[s, slot // GROUPS], dst_ref=fdrecv.at[s, back],
-            send_sem=fsend.at[s, slot], recv_sem=frecv.at[s, back],
-            device_id=plan.device(slot, me), device_id_type=MESH,
-        )
-
-    def each(make, s, act):
+    c_bufs = (lambda s, slot: sbuf.at[s], cbuf, csend, crecv)
+    f_bufs = (lambda s, slot: fdbuf.at[s, slot // GROUPS], fdrecv, fsend, frecv)
+
+    def start(bufs, s):
         for slot in plan.others:
-            when(plan.valid(slot, me), lambda slot=slot: act(make(s, slot)))
-
-    def arrive(make, s):
+            when(plan.valid(slot, me), lambda slot=slot: copy(bufs, s, slot, plan.mirror(slot)).start())
+
+    def arrive(bufs, s):
+        for slot in reversed(plan.others):
+            when(plan.valid(slot, me), lambda slot=slot: copy(bufs, s, slot, slot).wait_recv())
+
+    def sent(bufs, s):
         for slot in plan.others:
-            when(plan.valid(slot, me), lambda slot=slot: make(s, slot, True).wait_recv())
+            when(plan.valid(slot, me), lambda slot=slot: copy(bufs, s, slot, plan.mirror(slot)).wait_send())
 
     def pack_coefs(s):
         packed = cs[0:PACK, :]
@@ -192,42 +224,36 @@
             packed = jnp.where(group24 == j, rolled(cs[j * PACK:(j + 1) * PACK, :], BORDER * j), packed)
         sbuf[s] = packed
 
+    cs[0:COEF, :] = got("coef")
     pack_coefs(0)
-    pl.semaphore_wait(barrier, number)
-    each(c_copy, 0, lambda c: c.start())
 
     zero8 = jnp.zeros((8, LANES), F32)
     src[...] = jnp.zeros_like(src)
-    src[0:COEF, :] = source_ref[...]
+    src[0:COEF, :] = got("source")
+    ds[0:3, :] = got("dip")
     inj[...] = jnp.zeros_like(inj)
     ext[...] = zero8
-    ext[0:3, :] = ext_ref[...]
+    ext[0:3, :] = got("ext")
     tmp[...] = zero8
     ind[...] = jnp.zeros_like(ind)
-    ind[0:GRID, :] = ind_ref[...]
+    ind[0:GRID, :] = got("ind")
     zs[...] = jnp.zeros_like(zs)
     ws[...] = jnp.zeros_like(ws)
     hsq[...] = jnp.zeros_like(hsq)
-    hsq[0:GRID, 0:COEF] = harm_ref[...]
+    hsq[0:COEF, 0:GRID] = got("harm")
     pk[...] = jnp.zeros_like(pk)
     colb[...] = jnp.zeros_like(colb)
     edir[...] = jnp.zeros_like(edir)
     edirp[...] = jnp.zeros_like(edirp)
     stren[...] = jnp.zeros_like(stren)
 
-    def project_tables():
-        square = hsq[...]
-        high, low = split(square[0:GRID_PAD])
-        hk[:, 0:LANES] = high
-        hk[:, LANES:] = low
-        turned = square.T[0:ROWS]
-        lebedev = jnp.broadcast_to(leb_ref[...], (ROWS, GRID))
-        hsq[0:ROWS, :] = jnp.zeros((ROWS, LANES), F32)
-        return turned, lebedev
-
-    turned, lebedev = project_tables()
-    lebw = jnp.concatenate([lebedev, jnp.zeros((ROWS, GRID_K - GRID), F32)], axis=1)
-    weighted = turned * lebw
+    square = hsq[...]
+    high, low = split(square.T[0:GRID_PAD])
+    hk[:, 0:LANES] = high
+    hk[:, LANES:] = low
+    leb[...] = jnp.zeros_like(leb)
+    leb[0:1, 0:GRID] = got("leb").reshape(1, GRID)
+    weighted = square[0:ROWS] * jnp.broadcast_to(leb[0:1, :], (ROWS, GRID_K))
     high, low = split(weighted)
     ht[0:ROWS, :] = high
     ht[ROWS:, :] = low
@@ -236,24 +262,24 @@
     high3 = three.astype(BF16).astype(F32)
     htm[...] = jnp.concatenate([high3, three - high3], axis=0).astype(BF16)
 
-    live = jnp.where(lax.broadcasted_iota(jnp.int32, (1, LANES), 1) < counts_ref[0, 0], 1.0, 0.0)
+    live = jnp.where(lax.broadcasted_iota(jnp.int32, (1, LANES), 1) < jnp.broadcast_to(got("counts"), (1, LANES)), 1.0, 0.0)
     degrees = degree_rows(ROWS)
     gain = live * (2.0 * degrees + 1.0) / (4.0 * math.pi)
     degrees = degrees[0:CROWS]
 
-    column = columns(cidx_ref[...], me, plan)
-    weight = cw_ref[...]
-    dist = cd_ref[...]
-    sin_t = jnp.sin(ct_ref[...])
-    phi = cp_ref[...]
+    column = columns(got("cidx"), me, plan)
+    weight = got("cw")
+    dist = got("cd")
+    sin_t, cos_t = sine_cosine(got("ct"))
+    sin_p, cos_p = sine_cosine(got("cp"))
     colb[0:PAIRS, :] = column
     values = (
         weight,
         jnp.log(RADIUS_SCALE / dist),
         weight / (dist * dist * dist),
-        sin_t * jnp.cos(phi),
-        sin_t * jnp.sin(phi),
-        jnp.cos(ct_ref[...]),
+        sin_t * cos_p,
+        sin_t * sin_p,
+        cos_t,
     )
     for v, value in enumerate(values):
         pk[v, 0:PAIRS, :] = value
@@ -276,6 +302,9 @@
 
     def spread(row, rows):
         return jnp.broadcast_to(row, (rows, LANES))
+
+    pl.semaphore_wait(barrier, number)
+    start(c_bufs, 0)
 
     row128 = lax.broadcasted_iota(jnp.int32, (LANES, LANES), 0)
     for k in range(PAIRS):
@@ -292,15 +321,18 @@
         for c in range(3):
             edirp[g, c:c + 1, :] = value_p[3 + c][g:g + 1]
 
-    tcol = columns(tidx_ref[...], me, plan)
-    cubed = td_ref[...] * td_ref[...] * td_ref[...]
+    tcol = columns(got("tidx"), me, plan)
+    apart = got("td")
+    cubed = apart * apart * apart
     screen = jnp.exp(-THOLE_DAMPING * cubed)
-    scaled = tw_ref[...] / cubed
+    scaled = got("tw") / cubed
     lam3 = scaled * (1.0 - screen)
     lam5 = 3.0 * scaled * (1.0 - (1.0 + THOLE_DAMPING * cubed) * screen)
-    tsin = jnp.sin(tt_ref[...])
+    sin_t, cos_t = sine_cosine(got("tt"))
+    sin_p, cos_p = sine_cosine(got("tp"))
+    polar = live * got("polar")
     for v, value in enumerate((
-        tsin * jnp.cos(tp_ref[...]), tsin * jnp.sin(tp_ref[...]), jnp.cos(tt_ref[...]), lam3, lam5,
+        sin_t * cos_p, sin_t * sin_p, cos_t, lam3, lam5,
     )):
         thc[v] = value
     tlanes = tcol & (LANES - 1)
@@ -331,7 +363,7 @@
         for t in range(plan.tiles):
             part = away[:, t * LANES:(t + 1) * LANES]
             fdbuf[s, t] = jnp.where(iota8 < 3, part[0:8] + part[8:], dip_rows)
-        each(f_copy, s, lambda c: c.start())
+        start(f_bufs, s)
         mine = lax.dot_general(fown[...], ohown[...], turn, preferred_element_type=F32)
         return mine[0:8] + mine[8:]
 
@@ -355,7 +387,7 @@
         coupled = jnp.zeros((CROWS, LANES), F32)
         for k in range(PAIRS):
             coupled = coupled + wr[k] * lane_take(table, spread(lanes_own[k:k + 1], CROWS))
-        arrive(c_copy, s)
+        arrive(c_bufs, s)
         for t in range(plan.tiles):
             for j in range(GROUPS):
                 block = jnp.zeros((PACK, LANES), F32)
@@ -369,10 +401,10 @@
         for g in range(GROUPS):
             lanes = spread(lanes_rem[g:g + 1], CROWS)
             tiles = spread(tile_rem[g:g + 1], CROWS)
-            got = lane_take(pool[0, 0:CROWS, :], lanes)
+            found = lane_take(pool[0, 0:CROWS, :], lanes)
             for t in range(1, plan.tiles):
-                got = jnp.where(tiles == t + 1, lane_take(pool[t, 0:CROWS, :], lanes), got)
-            far = far + wrp[g] * got
+                found = jnp.where(tiles == t + 1, lane_take(pool[t, 0:CROWS, :], lanes), found)
+            far = far + wrp[g] * found
         far = far + rolled(far, 64)
         far = far + rolled(far, 32)
         coupled = coupled + jnp.where(lane_group((CROWS, LANES)) == 0, far, 0.0)
@@ -385,11 +417,11 @@
         if s < ITERS - 1:
             cs[...] = fresh
             pack_coefs(s + 1)
-            each(c_copy, s + 1, lambda c: c.start())
+            start(c_bufs, s + 1)
         else:
-            coef_out[...] = fresh[0:COEF]
-
-        arrive(f_copy, s)
+            coef_out[:, 0, :] = fresh[0:COEF]
+
+        arrive(f_bufs, s)
         reaction = own_field
         for m in range(GROUPS):
             total = None
@@ -409,38 +441,37 @@
             tables.append(block)
         partner = []
         for c in range(3):
-            got = jnp.zeros((PAIRS, LANES), F32)
+            found = jnp.zeros((PAIRS, LANES), F32)
             for t, block in enumerate(tables):
-                got = jnp.where(ttile == t, lane_take(spread(block[3 + c:4 + c], PAIRS), tlanes), got)
-            partner.append(got)
+                found = jnp.where(ttile == t, lane_take(spread(block[3 + c:4 + c], PAIRS), tlanes), found)
+            partner.append(found)
         along = thc[4] * (thc[0] * partner[0] + thc[1] * partner[1] + thc[2] * partner[2])
         for c in range(3):
             tmp[c:c + 1, :] = jnp.sum(thc[c] * along - thc[3] * partner[c], axis=0, keepdims=True)
-        moved = live * polar_ref[...] * (ext[...] + tmp[...] + reaction)
+        moved = polar * (ext[...] + tmp[...] + reaction)
         moved = jnp.where(iota8 < 3, moved, 0.0)
         if s < ITERS - 1:
             ds[...] = moved
         else:
-            dip_out[...] = moved[0:3]
+            dip_out[:, 0, :] = moved[0:3]
 
     for s in range(ITERS):
-        each(c_copy, s, lambda c: c.wait_send())
-        each(f_copy, s, lambda c: c.wait_send())
+        sent(c_bufs, s)
+        sent(f_bufs, s)
 
 
 def rows_of(x):
-    return x.reshape(x.shape[0], x.shape[-1])
+    shape = (x.shape[0], x.shape[-1]) if x.shape[0] % 8 == 0 else (x.shape[0], 1, x.shape[-1])
+    return x.reshape(shape)
 
 
 def local(plan, *args):
     (coef, dip, source, ind, polar, ext, counts, cidx, cw, cd, ct, cp,
      tidx, tw, td, tt, tp, harm, leb) = args
-    flat = [rows_of(x) for x in (coef, dip, source, ind)]
-    flat += [polar.reshape(1, LANES), rows_of(ext), counts.reshape(1, 1)]
-    flat += [rows_of(x) for x in (cidx, cw, cd, ct, cp, tidx, tw, td, tt, tp)]
-    flat += [harm, leb.reshape(1, GRID)]
+    flat = [rows_of(x) for x in (coef, dip, source, ind, cidx, cw, cd, ct, cp, tidx, tw, td, tt, tp, ext)]
+    flat += [polar.reshape(1, LANES), harm.T, leb, counts]
     vmem = pl.BlockSpec(memory_space=pltpu.VMEM)
-    smem = pl.BlockSpec(memory_space=pltpu.SMEM)
+    held = [pltpu.VMEM(x.shape, x.dtype) for x in flat]
     scratch = [
         ((ROWS, LANES), F32), ((8, LANES), F32), ((ROWS, LANES), F32), ((ROWS, LANES), F32),
         ((8, LANES), F32), ((8, LANES), F32),
@@ -452,19 +483,19 @@
         ((LANES, PAIRS * LANES), BF16), ((plan.tiles * LANES, GROUPS * LANES), BF16),
         ((16, PAIRS * LANES), BF16), ((16, GROUPS * LANES), BF16),
         ((GRID_PAD, 2 * LANES), BF16), ((2 * ROWS, GRID_K), BF16), ((16, GRID_K), BF16),
-        ((GRID_K, LANES), F32),
+        ((LANES, GRID_K), F32), ((8, GRID_K), F32),
         ((2 * LANES, 2 * LANES), BF16), ((GRID_K, 2 * LANES), BF16), ((GRID_PAD, LANES), F32),
         ((5, PAIRS, LANES), F32), ((plan.tiles, ROWS, LANES), F32),
     ]
-    semaphores = [pltpu.SemaphoreType.DMA((ITERS, plan.count))] * 4
+    semaphores = [pltpu.SemaphoreType.DMA((ITERS, plan.count))] * 4 + [pltpu.SemaphoreType.DMA((len(flat),))]
     coef_new, dip_new = pl.pallas_call(
         functools.partial(kernel, plan),
-        out_shape=(jax.ShapeDtypeStruct((COEF, LANES), F32), jax.ShapeDtypeStruct((3, LANES), F32)),
-        in_specs=[smem if i == 6 else vmem for i in range(len(flat))],
+        out_shape=(jax.ShapeDtypeStruct((COEF, 1, LANES), F32), jax.ShapeDtypeStruct((3, 1, LANES), F32)),
+        in_specs=[pl.BlockSpec(memory_space=pltpu.HBM)] * len(flat),
         out_specs=(vmem, vmem),
-        scratch_shapes=[pltpu.VMEM(shape, kind) for shape, kind in scratch] + semaphores,
+        scratch_shapes=held + [pltpu.VMEM(shape, kind) for shape, kind in scratch] + semaphores,
         compiler_params=pltpu.CompilerParams(
-            collective_id=0, has_side_effects=True, vmem_limit_bytes=32 * 1024 * 1024
+            collective_id=0, has_side_effects=True, vmem_limit_bytes=60 * 1024 * 1024
         ),
     )(*flat)
     return coef_new.reshape(coef.shape), dip_new.reshape(dip.shape)

time: 27.3 us -> 24.3 us (0.89)
  local copies, waits for them, and re-layouts: 5.09 us -> 1.97 us
  Pallas kernels: 20.5 us -> 20.8 us
    unnamed x32 -> x4, local copies, waits for them, and re-layouts: 4.4 us -> 1.97 us
    reshape x1 -> x0, local copies, waits for them, and re-layouts: 0.68 us -> none  [local(): flat += [harm, leb.reshape(1, GRID)]]
where the time goes in v2:
time: 24.3 us; the launch traced here: 24.1 us
  Pallas kernels  20.8 us (86%)
  local copies, waits for them, and re-layouts  1.97 us (8%)
  between operations  1.3 us (5%)
    pallas_call x1, Pallas kernels, local(): pl.pallas_call(functools.partial(kernel, plan), out_shape=(jax.ShapeDtype...  20.8 us
    unnamed x4, local copies, waits for them, and re-layouts  1.97 us

profile of v2, /device:TPU:0, one launch (start us, length us, event | category | flops | bytes accessed | tf_op | source)
XLA Modules:
  0.0 24.1 jit_solution(16365690233282664000)
XLA Ops:
  1.3 20.8 %shard_map.194 = (f32[81,1,128]{2,1,0:T(1,128)}, f32[3,1,128]{2,1,0:T(1,128)}) custom-call(f32[81,1,128]{2,1,0:T(1,128)} %bitcast.25, f32[3,1,128]{2,1,0:T(1,128)} %bitcast.38, f32[81,1,128]{2,1,0:T(1,128)} %bitcast.26, f32[302,1,128]{2,1,0:T(1,128)} %bitcast.23, s32[16,128]{1,0:T(8,128)} %bitcast.28, f32[16,128]{1,0:T(8,128)} %bitcast.29, ...), custom_call_target="tpu_custom_call" | custom-call | tf_op jit(solution)/shard_map/pallas_call | solution.py:491
  22.1 0.0 copy-start
  22.1 1.4 %copy.26 = f32[81,1,1,1,128]{4,3,2,1,0:T(1,128)} copy(f32[81,1,1,1,128]{4,3,2,1,0:T(1,128)} %bitcast.27) | data formatting | bytes 82944
  23.5 0.0 copy-done
  23.5 0.6 %copy.27 = f32[3,1,1,1,128]{4,3,2,1,0:T(1,128)} copy(f32[3,1,1,1,128]{4,3,2,1,0:T(1,128)S(1)} %bitcast.40) | data formatting | bytes 3072
Async XLA Ops:
  22.1 1.4 %copy-start = (f32[3,1,128]{2,1,0:T(1,128)S(1)}, f32[3,1,128]{2,1,0:T(1,128)}, u32[]{:S(2)}) copy-start(f32[3,1,128]{2,1,0:T(1,128)} %get-tuple-element.5) | copy-start | bytes 4612

commit v3 on v2

--- a/solution.py
+++ b/solution.py
@@ -490,7 +490,7 @@
     semaphores = [pltpu.SemaphoreType.DMA((ITERS, plan.count))] * 4 + [pltpu.SemaphoreType.DMA((len(flat),))]
     coef_new, dip_new = pl.pallas_call(
         functools.partial(kernel, plan),
-        out_shape=(jax.ShapeDtypeStruct((COEF, 1, LANES), F32), jax.ShapeDtypeStruct((3, 1, LANES), F32)),
+        out_shape=(pltpu.VMEM((COEF, 1, LANES), F32), pltpu.VMEM((3, 1, LANES), F32)),
         in_specs=[pl.BlockSpec(memory_space=pltpu.HBM)] * len(flat),
         out_specs=(vmem, vmem),
         scratch_shapes=held + [pltpu.VMEM(shape, kind) for shape, kind in scratch] + semaphores,

time: 24.3 us -> 22.8 us (0.938)
  local copies, waits for them, and re-layouts: 1.97 us -> 1.18 us
  Pallas kernels: 20.8 us -> 20.2 us
    unnamed x4 -> x2, local copies, waits for them, and re-layouts: 1.97 us -> 1.18 us
    pallas_call x1, Pallas kernels: 20.8 us -> 20.2 us  [local(): pl.pallas_call(functools.partial(kernel, plan), out_shape=(pltpu.VMEM((CO...]
where the time goes in v3:
time: 22.8 us; the launch traced here: 22.6 us
  Pallas kernels  20.2 us (89%)
  between operations  1.29 us (6%)
  local copies, waits for them, and re-layouts  1.18 us (5%)
    pallas_call x1, Pallas kernels, local(): pl.pallas_call(functools.partial(kernel, plan), out_shape=(pltpu.VMEM((CO...  20.2 us
    unnamed x2, local copies, waits for them, and re-layouts  1.18 us

profile of v3, /device:TPU:0, one launch (start us, length us, event | category | flops | bytes accessed | tf_op | source)
XLA Modules:
  0.0 22.6 jit_solution(17563066986319860577)
XLA Ops:
  1.3 20.2 %shard_map.194 = (f32[81,1,128]{2,1,0:T(1,128)S(1)}, f32[3,1,128]{2,1,0:T(1,128)S(1)}) custom-call(f32[81,1,128]{2,1,0:T(1,128)} %bitcast.27, f32[3,1,128]{2,1,0:T(1,128)} %bitcast.39, f32[81,1,128]{2,1,0:T(1,128)} %bitcast.28, f32[302,1,128]{2,1,0:T(1,128)} %bitcast.25, s32[16,128]{1,0:T(8,128)} %bitcast.29, f32[16,128]{1,0:T(8,128)} %bitcast.30, ...), custom_call_target="tpu_custom_call" | custom-call | tf_op jit(solution)/shard_map/pallas_call | solution.py:491
  21.5 0.6 %copy.25 = f32[81,1,1,1,128]{4,3,2,1,0:T(1,128)} copy(f32[81,1,1,1,128]{4,3,2,1,0:T(1,128)S(1)} %bitcast.23) | data formatting | bytes 82944
  22.1 0.6 %copy.26 = f32[3,1,1,1,128]{4,3,2,1,0:T(1,128)} copy(f32[3,1,1,1,128]{4,3,2,1,0:T(1,128)S(1)} %bitcast.24) | data formatting | bytes 3072
